TPU v7x, 128 devices: a whole 4x4x4 slice. The times are simulated.
128 devices in a mesh: ctx: 32 (over x, z, y_hi), fsdp: 4 (over y_lo, core).
Axes of the slice: x: 4, y: 4 (y_hi: 2, y_lo: 2; y = y_hi * 2 + y_lo), z: 4, core: 2. Of those that a mesh axis runs over, the one named last changes fastest.
Arguments:
- block_input: bfloat16 [4, 4096, 1024], P('fsdp', 'ctx'), may hold values from -6 to 6
- routes: int32 [4, 4096, 8], P('fsdp', 'ctx'), may hold values from 0 to 31, all different within a row; in each aligned block of 128 rows (0 to 127, 128 to 255, ..., all dimensions but the last counted through in order) at most 48 rows name the same one
- block_pairs: int32 [32], replicated, may hold values from 0 to 31, each once
- norm1_gain: bfloat16 [1024], P('fsdp'), may hold values from 0.5 to 1.5
- w_query: bfloat16 [1024, 1024], P('fsdp'), may hold values from -0.75 to 0.75
- w_key: bfloat16 [1024, 512], P('fsdp'), may hold values from -0.75 to 0.75
- w_value: bfloat16 [1024, 512], P('fsdp'), may hold values from -0.1875 to 0.1875
- w_out: bfloat16 [1024, 1024], P('fsdp'), may hold values from -4 to 4
- norm2_gain: bfloat16 [1024], P('fsdp'), may hold values from 0.5 to 1.5
- w_router: bfloat16 [1024, 32], P('fsdp'), may hold values from -0.09375 to 0.09375
- w_gate: bfloat16 [32, 1024, 512], P('ctx', 'fsdp'), may hold values from -0.1875 to 0.1875
- w_up: bfloat16 [32, 1024, 512], P('ctx', 'fsdp'), may hold values from -0.1875 to 0.1875
- w_down: bfloat16 [32, 512, 1024], P('ctx', 'fsdp'), may hold values from -4 to 4
- cotangent: bfloat16 [4, 4096, 1024], P('fsdp', 'ctx'), may hold values from -6 to 6
Outputs:
- block_output: bfloat16 [4, 4096, 1024], P('fsdp', 'ctx')
- input_grad: float32 [4, 4096, 1024], P('fsdp', 'ctx')
- norm1_gain_grad: float32 [1024], P('fsdp')
- w_query_grad: float32 [1024, 1024], P('fsdp')
- w_key_grad: float32 [1024, 512], P('fsdp')
- w_value_grad: float32 [1024, 512], P('fsdp')
- w_out_grad: float32 [1024, 1024], P('fsdp')
- norm2_gain_grad: float32 [1024], P('fsdp')
- w_router_grad: float32 [1024, 32], P('fsdp')
- w_gate_grad: float32 [32, 1024, 512], P('ctx', 'fsdp')
- w_up_grad: float32 [32, 1024, 512], P('ctx', 'fsdp')
- w_down_grad: float32 [32, 512, 1024], P('ctx', 'fsdp')
Inputs may be any that keep to these rules, and one draw needn't show every extreme that they name: `routes`: each row names 8 different experts; among the 128 rows of one device no expert is named more than 48 times, a bound that some block reaches. `block_pairs`: each number appears once. Index c of ctx holds, in this order, the blocks of half of 128 tokens numbered block_pairs[c] and 63 - block_pairs[c].
All inputs are finite; a program needn't handle non-finite values.
Results may differ from a plain program's by a relative error of at most 0.035.
Values may be sent and summed in bfloat16 or wider, within the bound.
No kernel may reach another device: no remote copies, remote signals or barrier semaphores. Data moves between devices by JAX's collectives and lax.ppermute only.
A program may use at most 128 MiB of HBM per device.

v0:
```python
import functools

import jax
import jax.numpy as jnp
from jax import lax
from jax.experimental import pallas as pl
from jax.experimental.layout import Layout, with_layout_constraint
from jax.experimental.pallas import tpu as pltpu
from jax.sharding import Mesh
from jax.sharding import PartitionSpec as P

HEADS = 16
KV_HEADS = 8
HEAD_DIM = 64
EXPERTS = 32
TOP = 8
CAP = 48
HALF = 64
TILE = 512

epsilon = 1e-06
attn_scale = 0.015625
residual_scale = 0.22
masked_value = -1e30

CTX = ("x", "z", "yh")
ZY = ("z", "yh")
EVERY = ("x", "z", "yh", "yl", "core")
bf16 = jnp.bfloat16
f32 = jnp.float32


def product(left, right):
    return jnp.dot(left, right, preferred_element_type=f32)


def product_nt(left, right):
    return lax.dot_general(left, right, (((1,), (1,)), ((), ())), preferred_element_type=f32)


def product_tn(left, right):
    return lax.dot_general(left, right, (((0,), (0,)), ((), ())), preferred_element_type=f32)


def swap(values, axis):
    return lax.ppermute(values, axis, [(0, 1), (1, 0)])


def turn(values, axis, step):
    return lax.ppermute(values, axis, [(i, (i + step) % 4) for i in range(4)])


def rows_first(values):
    return with_layout_constraint(values, Layout(major_to_minor=tuple(range(values.ndim))))


def exchange(values, axes):
    return rows_first(lax.all_to_all(rows_first(values), axes, 0, 0, tiled=True))


def tie(values, *others):
    if values.size <= 1024:
        return values + sum(other[(0,) * other.ndim].astype(f32) * 0.0 for other in others).astype(values.dtype)
    corner = tuple(slice(0, min(size, 8 if axis < values.ndim - 1 else 128)) for axis, size in enumerate(values.shape))
    nothing = sum(other[(0,) * other.ndim].astype(f32) * 0.0 for other in others)
    held = values[corner] + nothing.astype(values.dtype)
    return lax.dynamic_update_slice(values, held, (0,) * values.ndim)


def pieces_direct(shard):
    steps = [lax.ppermute(shard, ("yl", "core"), [(i, i ^ k) for i in range(4)]) for k in (1, 2, 3)]
    return (shard, *steps)


def pieces_by_row(shard, other):
    return (shard, swap(shard, "core"), other, swap(other, "core"))


def scatter_core(parts):
    core = lax.axis_index("core")
    parts = parts.astype(bf16).reshape((2, 2) + parts.shape[1:])
    away = lax.dynamic_index_in_dim(parts, 1 - core, 1, keepdims=False)
    keep = lax.dynamic_index_in_dim(parts, core, 1, keepdims=False)
    return (keep.astype(f32) + swap(away, "core").astype(f32)).astype(bf16)


def join_core(keep, away):
    return (keep.astype(f32) + swap(away, "core").astype(f32)).astype(bf16)


def scatter_row(both):
    row = lax.axis_index("yl")
    away = lax.dynamic_index_in_dim(both, 1 - row, 0, keepdims=False)
    keep = lax.dynamic_index_in_dim(both, row, 0, keepdims=False)
    return keep.astype(f32) + swap(away, "yl").astype(f32)


def scatter_fsdp(parts):
    return scatter_row(scatter_core(parts))


def all_x(part):
    return [part] + [turn(part, "x", step) for step in (1, 2, 3)]


def rope_tables(positions):
    freqs = jnp.power(10000.0, -jnp.arange(0, HEAD_DIM, 2, dtype=f32) / HEAD_DIM)
    angles = positions.astype(f32)[:, None] * freqs[None, :]
    cosine, sine = jnp.cos(angles), jnp.sin(angles)
    ones, zeros = jnp.ones_like(cosine), jnp.zeros_like(cosine)
    return (
        jnp.concatenate([cosine] * 6 + [ones] * 2, axis=1),
        jnp.concatenate([-sine, sine] * 3 + [zeros] * 2, axis=1),
    )


def turned(values):
    width = values.shape[1]
    column = lax.broadcasted_iota(jnp.int32, values.shape, 1)
    return jnp.where(
        column % HEAD_DIM < HEAD_DIM // 2,
        pltpu.roll(values, width - HEAD_DIM // 2, 1),
        pltpu.roll(values, HEAD_DIM // 2, 1),
    )


def norm_back(values, inv_rms, gain, grad):
    weighted = grad * gain
    gain_grad = jnp.sum(grad * values * inv_rms, axis=0, keepdims=True)
    inner_mean = jnp.mean(weighted * values, axis=-1, keepdims=True)
    return (weighted * inv_rms - values * inv_rms * inv_rms * inv_rms * inner_mean, gain_grad)


def inv_rms_of(values):
    return lax.rsqrt(jnp.mean(values * values, axis=-1, keepdims=True) + epsilon)


def half(index):
    return pl.ds(pl.multiple_of(index * HALF, HALF), HALF)


def key_tile(counter):
    return pl.ds(pl.multiple_of(counter * TILE, TILE), TILE)


def sort_keys(knum_ref, kv_refs, kvs, kvt):
    blocks = kv_refs[0].shape[0] // HALF
    for slot, kv_ref in enumerate(kv_refs):
        for block in range(blocks):
            kvs[half(knum_ref[slot * blocks + block]), :] = kv_ref[block * HALF : (block + 1) * HALF, :]
    for tile in range(kvs.shape[0] // TILE):
        part = kvs[tile * TILE : (tile + 1) * TILE, :].astype(f32)
        kvt[:, tile * TILE : (tile + 1) * TILE] = part.T.astype(bf16)


def pair_rows(ref, first, second, upper):
    rows = []
    for block in (first, second):
        values = ref[half(block), :].astype(f32)
        column = lax.broadcasted_iota(jnp.int32, values.shape, 1)
        inside = (column >= HEAD_DIM) if upper else (column < HEAD_DIM)
        moved = pltpu.roll(values, HEAD_DIM, 1)
        heads = (moved, values) if upper else (values, moved)
        rows += [jnp.where(inside, head, 0.0) for head in heads]
    return jnp.concatenate(rows, axis=0)


def pair_positions(low_number, high_number):
    column = lax.broadcasted_iota(jnp.int32, (1, 4 * HALF), 1)
    return jnp.where(column < 2 * HALF, low_number, high_number) * HALF + column % HALF


def score_tile(keys, queries, counter, positions, masked):
    scores = product_nt(keys, queries)
    if masked:
        key_pos = counter * TILE + lax.broadcasted_iota(jnp.int32, scores.shape, 0)
        scores = jnp.where(key_pos <= positions, scores, masked_value)
    return scores


def store_rows(ref, turned, first, second):
    rows = turned.T
    ref[half(first), :] = jnp.concatenate([rows[:HALF], rows[HALF : 2 * HALF]], axis=1).astype(ref.dtype)
    ref[half(second), :] = jnp.concatenate([rows[2 * HALF : 3 * HALF], rows[3 * HALF :]], axis=1).astype(ref.dtype)


def attend_kernel(
    order_ref, qnum_ref, knum_ref, q_ref, kv0, kv1, kv2, kv3, held_ref, out_ref, turned_ref, lse_ref, kvs, kvt
):
    del held_ref
    sort_keys(knum_ref, (kv0, kv1, kv2, kv3), kvs, kvt)
    width = 4 * HALF

    @pl.loop(0, q_ref.shape[0] // (2 * HALF))
    def _(pair):
        first, second = order_ref[2 * pair], order_ref[2 * pair + 1]
        low_number, high_number = qnum_ref[first], qnum_ref[second]
        queries = pair_rows(q_ref, first, second, False).astype(bf16)
        positions = pair_positions(low_number, high_number)

        def step(masked, counter, running):
            top, total, mixed = running
            scores = score_tile(kvs[key_tile(counter), :], queries, counter, positions, masked)
            new_top = jnp.maximum(top, jnp.max(scores, axis=0, keepdims=True))
            probs = jnp.exp(scores - new_top)
            shrink = jnp.exp(top - new_top)
            total = total * shrink + jnp.sum(probs, axis=0, keepdims=True)
            mixed = mixed * shrink + product(kvt[HEAD_DIM:, key_tile(counter)], probs.astype(bf16))
            return (new_top, total, mixed)

        start = (
            jnp.full((1, width), masked_value, f32),
            jnp.zeros((1, width), f32),
            jnp.zeros((HEAD_DIM, width), f32),
        )
        full = (low_number * HALF) // TILE
        last = (high_number * HALF) // TILE + 1
        running = lax.fori_loop(0, full, functools.partial(step, False), start)
        top, total, mixed = lax.fori_loop(full, last, functools.partial(step, True), running)
        mixed = mixed / total
        turned_ref[pair] = mixed
        lse_ref[pair] = top + jnp.log(total)
        store_rows(out_ref, mixed, first, second)


def attend_grad_kernel(
    order_ref, qnum_ref, knum_ref, q_ref, kv0, kv1, kv2, kv3, grad_ref, turned_ref, lse_ref,
    dq_ref, dkv0, dkv1, dkv2, dkv3, kvs, kvt, total_ref,
):
    sort_keys(knum_ref, (kv0, kv1, kv2, kv3), kvs, kvt)
    total_ref[...] = jnp.zeros_like(total_ref)
    width = 4 * HALF

    @pl.loop(0, q_ref.shape[0] // (2 * HALF))
    def _(pair):
        first, second = order_ref[2 * pair], order_ref[2 * pair + 1]
        low_number, high_number = qnum_ref[first], qnum_ref[second]
        queries = pair_rows(q_ref, first, second, False).astype(bf16)
        grads_f = pair_rows(grad_ref, first, second, True)
        grads = grads_f.astype(bf16)
        both = jnp.concatenate([queries, grads], axis=0)
        positions = pair_positions(low_number, high_number)
        lse = lse_ref[pair]
        dots = jnp.sum(grads_f.T[HEAD_DIM:] * turned_ref[pair], axis=0, keepdims=True)

        def step(masked, counter, query_acc):
            keys = kvs[key_tile(counter), :]
            probs = jnp.exp(score_tile(keys, queries, counter, positions, masked) - lse)
            score_grad = (probs * (product_nt(keys, grads) - dots)).astype(bf16)
            sides = jnp.concatenate([score_grad, probs.astype(bf16)], axis=1)
            total_ref[key_tile(counter), :] += product(sides, both)
            return query_acc + product(kvt[:HEAD_DIM, key_tile(counter)], score_grad)

        full = (low_number * HALF) // TILE
        last = (high_number * HALF) // TILE + 1
        query_acc = lax.fori_loop(0, full, functools.partial(step, False), jnp.zeros((HEAD_DIM, width), f32))
        query_acc = lax.fori_loop(full, last, functools.partial(step, True), query_acc)
        store_rows(dq_ref, query_acc * attn_scale, first, second)

    blocks = dkv0.shape[0] // HALF
    for slot, dkv in enumerate((dkv0, dkv1, dkv2, dkv3)):
        for block in range(blocks):
            dkv[block * HALF : (block + 1) * HALF, :] = total_ref[
                half(knum_ref[slot * blocks + block]), :
            ].astype(bf16)


def expert_kernel(
    expert_ref, me_ref, rows_ref, marked_ref, piece0, piece1, piece2, piece3, router_ref,
    out_ref, in_grad_ref, pre_grad_ref, inner_ref, route_grad_ref, gu_ref, down_ref,
):
    @pl.when(pl.program_id(0) == 0)
    def _():
        part = gu_ref.shape[0] // 4
        for step, piece in enumerate((piece0, piece1, piece2, piece3)):
            place = me_ref[0] ^ step
            gu_ref[pl.ds(pl.multiple_of(place * part, part), part), :] = piece[:part, :]
            down_ref[pl.ds(pl.multiple_of(place * (part // 2), part // 2), part // 2), :] = piece[part:, :]

    rows = rows_ref[...]
    width = rows.shape[1]
    units = down_ref.shape[0]
    pre = product(rows, gu_ref[...])
    gate_pre, up_pre = pre[:, :units], pre[:, units:]
    sigmoid_a = 1.0 / (1.0 + jnp.exp(-gate_pre))
    swish_act = gate_pre * sigmoid_a
    inner_act = (swish_act * up_pre).astype(bf16)
    inner_ref[...] = inner_act
    expert_out = product(inner_act, down_ref[...]).astype(bf16)
    out_ref[...] = expert_out
    uses = marked_ref[:, width : width + EXPERTS].astype(f32)
    probs = gate_of(rows, uses, router_ref[...])
    column = lax.broadcasted_iota(jnp.int32, probs.shape, 1)
    slot_probs = jnp.sum(jnp.where(column == expert_ref[0], probs, 0.0), axis=1, keepdims=True)
    mix_grad = residual_scale * marked_ref[:, :width].astype(f32)
    gate_grad = jnp.sum(mix_grad * expert_out.astype(f32), axis=1, keepdims=True)
    route_grad = (slot_probs * mix_grad).astype(bf16)
    route_grad_ref[...] = route_grad
    inner_grad = product_nt(route_grad, down_ref[...])
    pre_grad_ref[:, :units] = (
        inner_grad * up_pre * sigmoid_a * (1.0 + gate_pre * (1.0 - sigmoid_a))
    ).astype(bf16)
    pre_grad_ref[:, units:] = (inner_grad * swish_act).astype(bf16)
    in_grad_ref[:, :width] = product_nt(pre_grad_ref[...], gu_ref[...]).astype(bf16)
    column = lax.broadcasted_iota(jnp.int32, (rows.shape[0], 128), 1)
    high = gate_grad.astype(bf16).astype(f32)
    in_grad_ref[:, width:] = jnp.where(
        column == expert_ref[0], high, jnp.where(column == EXPERTS + expert_ref[0], gate_grad - high, 0.0)
    ).astype(bf16)


def project_kernel(x_ref, w_ref, gain_ref, cos_ref, sin_ref, normed_ref, q_ref, kv_ref):
    values = x_ref[...].astype(f32)
    normed = (values * inv_rms_of(values) * gain_ref[...]).astype(bf16)
    normed_ref[...] = normed
    projected = product(normed, w_ref[...])
    rotated = projected * cos_ref[...] + turned(projected) * sin_ref[...]
    q_ref[...] = rotated[:, : 2 * HEAD_DIM].astype(bf16) * bf16(attn_scale)
    kv_ref[...] = rotated[:, 2 * HEAD_DIM :].astype(bf16)


def project(rows, head_w, gain, cosine, sine):
    count, width = rows.shape
    tile = 256

    def tiled(columns):
        return pl.BlockSpec((tile, columns), lambda i: (i, 0))

    def whole(array):
        return pl.BlockSpec(array.shape, lambda i: (0, 0))

    columns = (width, 2 * HEAD_DIM, 2 * HEAD_DIM)
    return pl.pallas_call(
        project_kernel,
        grid=(count // tile,),
        out_shape=tuple(jax.ShapeDtypeStruct((count, c), bf16) for c in columns),
        in_specs=[tiled(width), whole(head_w), whole(gain), tiled(4 * HEAD_DIM), tiled(4 * HEAD_DIM)],
        out_specs=tuple(tiled(c) for c in columns),
        compiler_params=pltpu.CompilerParams(vmem_limit_bytes=32 * 1024 * 1024),
        cost_estimate=pl.CostEstimate(flops=600_000_000, bytes_accessed=8_000_000, transcendentals=0),
    )(rows, head_w, gain, cosine, sine)


def call(kernel, outs, operands, flops, held=(), scalars=0, scratch=()):
    count = len(operands)

    def body(*refs):
        kernel(*refs[:count], *refs[count + len(held) :])

    return pl.pallas_call(
        body,
        out_shape=tuple(jax.ShapeDtypeStruct(shape, dtype) for shape, dtype in outs),
        in_specs=[SMEM] * scalars + [VMEM] * (count - scalars) + [pl.BlockSpec(memory_space=pl.ANY)] * len(held),
        out_specs=(VMEM,) * len(outs),
        scratch_shapes=[pltpu.VMEM(shape, f32) for shape in scratch],
        compiler_params=pltpu.CompilerParams(vmem_limit_bytes=48 * 1024 * 1024),
        cost_estimate=pl.CostEstimate(flops=flops, bytes_accessed=8_000_000, transcendentals=0),
    )(*operands, *held)


def part_of(me_ref, step, part):
    return pl.ds(pl.multiple_of((me_ref[0] ^ step) * part, part), part)


def copies_kernel(x_ref, copies_ref):
    for copy in range(KV_HEADS):
        copies_ref[copy] = x_ref[...]


def shard_kernel(head_ref, query_ref, key_ref, value_ref, router_ref, gain1_ref, gain2_ref, out_ref):
    rows = query_ref.shape[0]
    head = head_ref[0]
    out_ref[...] = jnp.zeros_like(out_ref)
    out_ref[:rows, : 2 * HEAD_DIM] = query_ref[:, pl.ds(pl.multiple_of(head * 128, 128), 128)]
    pair = pl.ds(pl.multiple_of((head // 2) * 128, 128), 128)
    odd = jnp.full((rows, 128), head % 2, jnp.int32) == 1
    column = lax.broadcasted_iota(jnp.int32, (rows, 128), 1)
    keys, values = key_ref[:, pair].astype(f32), value_ref[:, pair].astype(f32)
    keys = jnp.where(odd, pltpu.roll(keys, HEAD_DIM, 1), keys)
    values = jnp.where(odd, values, pltpu.roll(values, HEAD_DIM, 1))
    out_ref[:rows, 2 * HEAD_DIM : 4 * HEAD_DIM] = jnp.where(column < HEAD_DIM, keys, values).astype(bf16)
    out_ref[:rows, 4 * HEAD_DIM : 4 * HEAD_DIM + EXPERTS] = router_ref[...]
    row = lax.broadcasted_iota(jnp.int32, (16, rows), 0)
    gains = jnp.where(row == 0, gain1_ref[...].astype(f32), jnp.where(row == 1, gain2_ref[...].astype(f32), 0.0))
    out_ref[rows:, :rows] = gains.astype(bf16)


def small_kernel(me_ref, piece0, piece1, piece2, piece3, head_w_ref, router_ref, gain1_ref, gain2_ref):
    rows = head_w_ref.shape[0] // 4
    for step, piece in enumerate((piece0, piece1, piece2, piece3)):
        place = part_of(me_ref, step, rows)
        head_w_ref[place, :] = piece[:rows, : 4 * HEAD_DIM]
        router_ref[place, :] = piece[:rows, 4 * HEAD_DIM : 4 * HEAD_DIM + EXPERTS]
        gains = piece[rows:, :rows].astype(f32)
        gain1_ref[:, place] = gains[0:1]
        gain2_ref[:, place] = gains[1:2]


def send_kernel(send_ref, rows_ref, out_ref):
    out_ref[...] = product(send_ref[...], rows_ref[...]).astype(bf16)


def middle_kernel(
    me_ref, attn_ref, out0, out1, out2, out3, x_ref, gain_ref, router_ref, uses_ref, send_ref,
    rows_ref, hidden_ref, normed_ref, probs_ref, out_ref,
):
    for head in range(KV_HEADS):
        rows_ref[:, head * 2 * HEAD_DIM : (head + 1) * 2 * HEAD_DIM] = attn_ref[head]
    branch = jnp.zeros(hidden_ref.shape, f32)
    for step, piece in enumerate((out0, out1, out2, out3)):
        branch += product(rows_ref[:, part_of(me_ref, step, piece.shape[0])], piece[...])
    hidden = x_ref[...].astype(f32) + residual_scale * branch
    hidden_ref[...] = hidden
    normed = (hidden * inv_rms_of(hidden) * gain_ref[...]).astype(bf16)
    normed_ref[...] = normed
    out_ref[...] = product(send_ref[...], normed).astype(bf16)
    probs_ref[...] = gate_of(normed, uses_ref[...], router_ref[...])


def token_grad_kernel(
    me_ref, fetch_ref, back_ref, probs_ref, router_ref, hidden_ref, gain_ref, cot_ref, out0, out1, out2, out3,
    hidden_grad_ref, branch_ref, logit_ref, gain_grad_ref, attn_grad_ref,
):
    width = hidden_ref.shape[1]
    fetched = product(fetch_ref[...], back_ref[...])
    gate_grad = fetched[:, width : width + EXPERTS] + fetched[:, width + EXPERTS : width + 2 * EXPERTS]
    probs = probs_ref[...]
    mean_grad = jnp.sum(probs * gate_grad, axis=-1, keepdims=True)
    logit_grad = (probs * (gate_grad - mean_grad)).astype(bf16)
    logit_ref[...] = logit_grad
    normed_grad = fetched[:, :width] + product_nt(logit_grad, router_ref[...])
    hidden = hidden_ref[...]
    hidden_part, gain_grad = norm_back(hidden, inv_rms_of(hidden), gain_ref[...], normed_grad)
    gain_grad_ref[...] = gain_grad
    hidden_grad = cot_ref[...].astype(f32) + hidden_part
    hidden_grad_ref[...] = hidden_grad
    branch = (residual_scale * hidden_grad).astype(bf16)
    branch_ref[...] = branch
    for step, piece in enumerate((out0, out1, out2, out3)):
        attn_grad = product_nt(branch, piece[...]).astype(bf16)
        heads = KV_HEADS // 4
        for head in range(heads):
            columns = slice(head * 2 * HEAD_DIM, (head + 1) * 2 * HEAD_DIM)
            attn_grad_ref[(me_ref[0] ^ step) * heads + head] = attn_grad[:, columns]


def dense_grad_kernel(core_ref, rows_ref, branch_ref, normed_ref, logit_ref, gain_ref, keep_ref, away_ref):
    part, width = keep_ref.shape[1], branch_ref.shape[1]
    logit_grad = logit_ref[...].astype(f32)
    logit_grad = jnp.concatenate(
        [logit_grad, jnp.zeros((logit_grad.shape[0], 128 - EXPERTS), f32)], axis=1
    ).astype(bf16)
    column = lax.broadcasted_iota(jnp.int32, (part, 128), 1)
    for row in range(2):
        for ref, core in ((keep_ref, core_ref[0]), (away_ref, 1 - core_ref[0])):
            columns = pl.ds(pl.multiple_of((2 * row + core) * part, part), part)
            ref[row, :, :width] = product_tn(rows_ref[:, columns], branch_ref[...]).astype(bf16)
            router_grad = product_tn(normed_ref[:, columns], logit_grad)
            gain_grad = jnp.broadcast_to(gain_ref[:, columns], (128, part)).T
            ref[row, :, width:] = jnp.where(column == EXPERTS, gain_grad, router_grad).astype(bf16)


def head_grad_kernel(dq_ref, dkv0, dkv1, dkv2, dkv3, cos_ref, sin_ref, out_ref):
    dkv = dkv0[...].astype(f32) + dkv1[...].astype(f32) + dkv2[...].astype(f32) + dkv3[...].astype(f32)
    for side, grad in enumerate((dq_ref[...], dkv)):
        columns = slice(side * 2 * HEAD_DIM, (side + 1) * 2 * HEAD_DIM)
        out_ref[:, columns] = (grad * cos_ref[:, columns] - turned(grad) * sin_ref[:, columns]).astype(bf16)


def head_weight_kernel(core_ref, normed_ref, grads_ref, keep_ref, away_ref):
    part = keep_ref.shape[1]
    for row in range(2):
        for ref, core in ((keep_ref, core_ref[0]), (away_ref, 1 - core_ref[0])):
            columns = pl.ds(pl.multiple_of((2 * row + core) * part, part), part)
            ref[row] = product_tn(normed_ref[:, columns], grads_ref[...]).astype(bf16)


def input_grad_kernel(
    me_ref, grads_ref, w0, w1, w2, w3, x_ref, gain_ref, hidden_grad_ref, out_ref, gain0, gain1, gain2, gain3, all_ref
):
    width = 4 * HEAD_DIM
    for step, piece in enumerate((w0, w1, w2, w3)):
        part = jnp.zeros((out_ref.shape[0], piece.shape[0]), f32)
        for head in range(KV_HEADS):
            part += product_nt(grads_ref[head], piece[:, head * width : (head + 1) * width])
        out_ref[:, part_of(me_ref, step, piece.shape[0])] = part
    values = x_ref[...].astype(f32)
    part, gain_grad = norm_back(values, inv_rms_of(values), gain_ref[...], out_ref[...])
    out_ref[...] = hidden_grad_ref[...] + part
    all_ref[...] = gain_grad
    for step, ref in enumerate((gain0, gain1, gain2, gain3)):
        ref[...] = all_ref[:, part_of(me_ref, step, ref.shape[1])]


def pack_kernel(
    place_ref, w0, w1, w2, w3, gain0, gain1, gain2, gain3, dense0, dense1, dense2, dense3, out_ref, rows_ref
):
    total = w0[...].astype(f32) + w1[...].astype(f32) + w2[...].astype(f32) + w3[...].astype(f32)
    total = total.astype(bf16)
    gain = gain0[...] + gain1[...] + gain2[...] + gain3[...]
    high = gain.astype(bf16).astype(f32)
    rows, columns = total.shape[0] // 4, total.shape[1]
    row = lax.broadcasted_iota(jnp.int32, (rows, 128), 0)
    block = jnp.zeros((rows, 128), f32)
    for line, part in enumerate((high[:, :128], high[:, 128:], (gain - high)[:, :128], (gain - high)[:, 128:])):
        block = jnp.where(row == line, part, block)
    for step, part in enumerate((dense0, dense1, dense2, dense3)):
        rows_ref[pl.ds(pl.multiple_of(((place_ref[0] + 4 - step) & 3) * 8, 8), 8), :] = part[...].astype(f32)
    dense = rows_ref[...].astype(bf16)
    for head in range(KV_HEADS):
        for side in range(4):
            out_ref[head, :rows, side * columns : (side + 1) * columns] = total[side * rows : (side + 1) * rows]
        out_ref[head, :rows, 4 * columns :] = block.astype(bf16)
        out_ref[head, rows:, :] = dense


def spread_kernel(
    last_ref, query_ref, key_ref, value_ref, gain_ref, out_grad_ref, router_ref, gain2_ref, column_ref
):
    columns = 4 * HEAD_DIM
    rows = last_ref.shape[1] - 32
    gain_lines = jnp.zeros((rows, 128), f32)
    for head in range(0, KV_HEADS, 2):
        for side in range(4):
            place = slice(side * rows, (side + 1) * rows)
            parts = []
            for step in (0, 1):
                part = last_ref[head + step, :rows, side * columns : (side + 1) * columns].astype(f32)
                query_ref[place, (head + step) * 2 * HEAD_DIM : (head + step + 1) * 2 * HEAD_DIM] = part[:, : 2 * HEAD_DIM]
                parts.append(part)
            pair = slice(head * HEAD_DIM, (head + 2) * HEAD_DIM)
            key_ref[place, pair] = jnp.concatenate([p[:, 2 * HEAD_DIM : 3 * HEAD_DIM] for p in parts], axis=1)
            value_ref[place, pair] = jnp.concatenate([p[:, 3 * HEAD_DIM :] for p in parts], axis=1)
    for head in range(KV_HEADS):
        gain_lines += last_ref[head, :rows, 4 * columns :].astype(f32)
        dense = last_ref[head, rows:, :].astype(f32)
        for place in range(4):
            part = dense[place * 8 : (place + 1) * 8]
            target = slice((place * KV_HEADS + head) * 8, (place * KV_HEADS + head + 1) * 8)
            out_grad_ref[target, :] = part[:, : 4 * columns]
            router_ref[target, :] = part[:, 4 * columns : 4 * columns + EXPERTS]
            column_ref[target, :] = part[:, 4 * columns :]
    gain_ref[:, :128] = gain_lines[0:1] + gain_lines[2:3]
    gain_ref[:, 128:] = gain_lines[1:2] + gain_lines[3:4]
    gain2_ref[...] = column_ref[...].T[EXPERTS : EXPERTS + 1, :]


def gate_of(rows, mask, router_w):
    logits = jnp.where(mask > 0, product(rows, router_w), masked_value)
    exps = jnp.where(mask > 0, jnp.exp(logits - jnp.max(logits, axis=-1, keepdims=True)), 0.0)
    return exps / jnp.maximum(jnp.sum(exps, axis=-1, keepdims=True), 1e-30)


def run_experts(expert, me, rows, marked, pieces, router_w):
    count, width = rows.shape
    part = pieces[0].shape[0] // 3
    units = 4 * part
    tile = 256

    def tiled(columns):
        return pl.BlockSpec((tile, columns), lambda i: (i, 0))

    def whole(array):
        return pl.BlockSpec(array.shape, lambda i: (0, 0))

    columns = (width, width + 128, 2 * units, units, width)
    return pl.pallas_call(
        expert_kernel,
        grid=(count // tile,),
        out_shape=tuple(jax.ShapeDtypeStruct((count, c), bf16) for c in columns),
        in_specs=[SMEM, SMEM, tiled(width), tiled(width + 128)] + [whole(p) for p in pieces] + [whole(router_w)],
        out_specs=tuple(tiled(c) for c in columns),
        scratch_shapes=[pltpu.VMEM((8 * part, 2 * units), bf16), pltpu.VMEM((units, width), bf16)],
        compiler_params=pltpu.CompilerParams(vmem_limit_bytes=56 * 1024 * 1024),
        cost_estimate=pl.CostEstimate(flops=10_000_000_000, bytes_accessed=22_000_000, transcendentals=1_000_000),
    )(expert.astype(jnp.int32).reshape(1), me, rows, marked, *pieces, router_w)


SMEM = pl.BlockSpec(memory_space=pltpu.SMEM)
VMEM = pl.BlockSpec(memory_space=pltpu.VMEM)


def attend(numbers, queries, kv_parts, held):
    rows = queries.shape[0]
    keys = rows * len(kv_parts)
    pairs = rows // (2 * HALF)
    return pl.pallas_call(
        attend_kernel,
        out_shape=(
            jax.ShapeDtypeStruct((rows, 2 * HEAD_DIM), bf16),
            jax.ShapeDtypeStruct((pairs, HEAD_DIM, 4 * HALF), f32),
            jax.ShapeDtypeStruct((pairs, 1, 4 * HALF), f32),
        ),
        in_specs=[SMEM] * 3 + [VMEM] * 5 + [pl.BlockSpec(memory_space=pl.ANY)],
        out_specs=(VMEM,) * 3,
        scratch_shapes=[pltpu.VMEM((keys, 2 * HEAD_DIM), bf16), pltpu.VMEM((2 * HEAD_DIM, keys), bf16)],
        compiler_params=pltpu.CompilerParams(vmem_limit_bytes=40 * 1024 * 1024),
        cost_estimate=pl.CostEstimate(flops=12_000_000_000, bytes_accessed=4_000_000, transcendentals=5_000_000),
    )(*numbers, queries, *kv_parts, held)


def attend_grad(numbers, queries, kv_parts, grads, turned, lse):
    rows = queries.shape[0]
    keys = rows * len(kv_parts)
    return pl.pallas_call(
        attend_grad_kernel,
        out_shape=(jax.ShapeDtypeStruct((rows, 2 * HEAD_DIM), f32),)
        + (jax.ShapeDtypeStruct((rows, 2 * HEAD_DIM), bf16),) * 4,
        in_specs=[SMEM] * 3 + [VMEM] * 8,
        out_specs=(VMEM,) * 5,
        scratch_shapes=[
            pltpu.VMEM((keys, 2 * HEAD_DIM), bf16),
            pltpu.VMEM((2 * HEAD_DIM, keys), bf16),
            pltpu.VMEM((keys, 2 * HEAD_DIM), f32),
        ],
        compiler_params=pltpu.CompilerParams(vmem_limit_bytes=40 * 1024 * 1024),
        cost_estimate=pl.CostEstimate(flops=30_000_000_000, bytes_accessed=6_000_000, transcendentals=5_000_000),
    )(*numbers, queries, *kv_parts, grads, turned, lse)


def block_numbers(block_pairs):
    place = lax.axis_index("x")
    groups = block_pairs.reshape(4, 8)
    groups = groups[(place - jnp.arange(4)) & 3]
    numbers = jnp.stack([groups, 63 - groups], axis=-1).reshape(-1)
    own = numbers[:16]
    rank = jnp.sum((own[None, :] < own[:, None]).astype(jnp.int32), axis=1)
    spots = jnp.arange(16, dtype=jnp.int32)
    order = jnp.sum(jnp.where(rank[None, :] == spots[:, None], spots[None, :], 0), axis=1)
    return (order, own, numbers)


def on_device(
    block_input,
    routes,
    block_pairs,
    norm1_gain,
    w_query,
    w_key,
    w_value,
    w_out,
    norm2_gain,
    w_router,
    w_gate,
    w_up,
    w_down,
    cotangent,
):
    tokens, width = block_input.shape[1:]
    head = lax.axis_index(ZY)
    expert = lax.axis_index(CTX)
    shard_rows = w_query.shape[0]
    own_input = block_input[0]

    core = lax.axis_index("core").astype(jnp.int32).reshape(1)
    place = lax.axis_index("x").astype(jnp.int32).reshape(1)
    me = lax.axis_index(("yl", "core")).astype(jnp.int32).reshape(1)
    (small_shard,) = call(
        shard_kernel,
        [((shard_rows + 16, 4 * HEAD_DIM + 128), bf16)],
        (
            head.astype(jnp.int32).reshape(1), w_query, w_key, w_value, w_router,
            norm1_gain.reshape(1, -1), norm2_gain.reshape(1, -1),
        ),
        1_000_000,
        scalars=1,
    )
    small_pieces = pieces_direct(small_shard)
    (copies,) = call(
        copies_kernel, [((KV_HEADS, tokens, width), bf16)], (own_input,), 1_000_000, held=(small_shard,)
    )
    group_input = exchange(copies.reshape(-1, width), ZY)
    head_w, router_w, gain_one, gain_two = call(
        small_kernel,
        [((width, 4 * HEAD_DIM), bf16), ((width, EXPERTS), bf16), ((1, width), f32), ((1, width), f32)],
        (me, *small_pieces),
        1_000_000,
        scalars=1,
    )

    numbers = block_numbers(block_pairs)
    group_pos = (numbers[1][:, None] * HALF + jnp.arange(HALF, dtype=jnp.int32)[None, :]).reshape(-1)
    cosine, sine = rope_tables(group_pos)

    chosen = routes[0]
    uses = jnp.sum(
        (chosen[:, :, None] == jnp.arange(EXPERTS, dtype=jnp.int32)[None, None, :]).astype(f32), axis=1
    )
    earlier = jnp.tril(jnp.ones((tokens, tokens), bf16), -1)
    rank = product(earlier, uses.astype(bf16)).astype(jnp.int32)
    rank = jnp.where(uses > 0, rank, -1)
    slot = jnp.arange(CAP, dtype=jnp.int32)
    send = (rank.T[:, None, :] == slot[None, :, None]).astype(bf16).reshape(EXPERTS * CAP, tokens)
    fetch = (rank[:, :, None] == slot[None, None, :]).astype(bf16).reshape(tokens, EXPERTS * CAP)

    group_normed, queries, kv_own = project(group_input, head_w, gain_one, cosine, sine)
    kv_parts = [kv_own] + [turn(kv_own, "x", step) for step in (1, 2, 3)]

    out_other = swap(w_out, "yl")
    expert_shard = jnp.concatenate([jnp.concatenate([w_gate[0], w_up[0]], axis=1), w_down[0]], axis=0)
    expert_other = swap(expert_shard, "yl")
    marked = jnp.concatenate(
        [cotangent[0], uses.astype(bf16), jnp.zeros((tokens, 128 - EXPERTS), bf16)], axis=1
    )
    (marked_sent,) = call(
        send_kernel,
        [((EXPERTS * CAP, width + 128), bf16)],
        (send, marked),
        500_000_000,
        held=(*kv_parts[1:], out_other, expert_other),
    )
    marked_arrived = exchange(marked_sent, CTX)

    attn_group, attn_turned, lse = attend(numbers, queries, kv_parts, expert_other)

    out_pieces = pieces_by_row(w_out, out_other)

    attn_back = exchange(tie(attn_group, marked_arrived), ZY)
    expert_pieces = pieces_by_row(expert_shard, expert_other)
    attn_rows, hidden, normed2, gate_probs, outgoing = call(
        middle_kernel,
        [
            ((tokens, HEADS * HEAD_DIM), bf16),
            ((tokens, width), f32),
            ((tokens, width), bf16),
            ((tokens, EXPERTS), f32),
            ((EXPERTS * CAP, width), bf16),
        ],
        (
            me, attn_back.reshape(KV_HEADS, tokens, 2 * HEAD_DIM), *out_pieces, own_input, gain_two, router_w,
            uses, send,
        ),
        800_000_000,
        held=expert_pieces,
        scalars=1,
    )
    arrived = exchange(outgoing, CTX)

    hidden_units = w_gate.shape[2]
    expert_out, in_grad, pre_grad, inner_act, route_grad = run_experts(
        expert, me, arrived, marked_arrived, expert_pieces, router_w
    )
    back = exchange(in_grad, CTX)
    grad_gu = product_tn(arrived, pre_grad).astype(bf16).reshape(4, -1, 2 * hidden_units)
    grad_down = product_tn(inner_act, route_grad).astype(bf16).reshape(4, -1, width)
    expert_both = scatter_core(jnp.concatenate([grad_gu, grad_down], axis=1))
    by_head = jnp.concatenate(
        [
            w_query.reshape(shard_rows, KV_HEADS, 2 * HEAD_DIM),
            w_key.reshape(shard_rows, KV_HEADS, HEAD_DIM),
            w_value.reshape(shard_rows, KV_HEADS, HEAD_DIM),
        ],
        axis=2,
    ).reshape(shard_rows, -1)
    by_head = tie(by_head, arrived)
    head_pieces = pieces_by_row(by_head, swap(by_head, "yl"))
    expert_sums = scatter_row(expert_both)

    hidden_grad, branch_grad, logit_grad, gain_two_grad, attn_grad = call(
        token_grad_kernel,
        [
            ((tokens, width), f32),
            ((tokens, width), bf16),
            ((tokens, EXPERTS), bf16),
            ((1, width), f32),
            ((KV_HEADS, tokens, 2 * HEAD_DIM), bf16),
        ],
        (me, fetch, back, gate_probs, router_w, hidden, gain_two, cotangent[0], *out_pieces),
        800_000_000,
        held=(expert_sums, *head_pieces),
        scalars=1,
    )

    group_grad = exchange(attn_grad.reshape(KV_HEADS * tokens, 2 * HEAD_DIM), ZY)
    dq, *dkv_parts = attend_grad(numbers, queries, kv_parts, group_grad, attn_turned, lse)
    returned = exchange(tie(expert_out, group_grad), CTX)
    dkv_turned = [turn(dkv_parts[step], "x", -step) for step in (1, 2, 3)]
    dense_shape = ((2, shard_rows, width + 128), bf16)
    dense_both = join_core(
        *call(
            dense_grad_kernel,
            [dense_shape, dense_shape],
            (core, attn_rows, branch_grad, normed2, logit_grad, gain_two_grad),
            400_000_000,
            held=tuple(dkv_turned),
            scalars=1,
        )
    )
    dense = scatter_row(dense_both)

    (grads,) = call(
        head_grad_kernel,
        [((KV_HEADS * tokens, 4 * HEAD_DIM), bf16)],
        (dq, dkv_parts[0], *dkv_turned, cosine, sine),
        100_000_000,
        held=(returned,),
    )
    token_grads = exchange(grads, ZY)
    head_shape = ((2, shard_rows, 4 * HEAD_DIM), bf16)
    head_both = join_core(
        *call(head_weight_kernel, [head_shape, head_shape], (core, group_normed, grads), 600_000_000, scalars=1)
    )
    head_part = scatter_row(head_both).astype(bf16)

    dense = exchange(tie(dense.astype(bf16), token_grads, head_part), CTX).reshape(EXPERTS, -1, width + 128)
    dense = jnp.sum(dense.astype(f32), axis=0).astype(bf16)

    gain_shape = ((1, shard_rows), f32)
    input_grad, *gain_parts = call(
        input_grad_kernel,
        [((tokens, width), f32)] + [gain_shape] * 4,
        (
            me, token_grads.reshape(KV_HEADS, tokens, 4 * HEAD_DIM), *head_pieces, own_input, gain_one, hidden_grad,
        ),
        600_000_000,
        scalars=1,
        scratch=[(1, width)],
    )
    gain_sum = gain_parts[0]
    for step in (1, 2, 3):
        gain_sum = gain_sum + lax.ppermute(gain_parts[step], ("yl", "core"), [(i, i ^ step) for i in range(4)])

    (last,) = call(
        pack_kernel,
        [((KV_HEADS, shard_rows // 4 + 32, width + 128), bf16)],
        (place, *all_x(tie(head_part, gain_parts[0])), *all_x(tie(gain_sum, dense)), *all_x(dense)),
        1_000_000,
        scalars=1,
        scratch=[(32, width + 128)],
    )
    last = exchange(last.reshape(-1, width + 128), ZY).reshape(last.shape)
    grad_query, grad_key, grad_value, gain_one_grad, grad_out, grad_router, gain_two_grad = call(
        spread_kernel,
        [
            ((shard_rows, HEADS * HEAD_DIM), f32),
            ((shard_rows, KV_HEADS * HEAD_DIM), f32),
            ((shard_rows, KV_HEADS * HEAD_DIM), f32),
            gain_shape,
            ((shard_rows, width), f32),
            ((shard_rows, EXPERTS), f32),
            gain_shape,
        ],
        (last,),
        1_000_000,
        scratch=[(shard_rows, 128)],
    )

    spread = gate_probs[:, :, None] * fetch.astype(f32).reshape(tokens, EXPERTS, CAP)
    weights = spread.reshape(tokens, EXPERTS * CAP)
    weights_hi = weights.astype(bf16)
    weights_lo = (weights - weights_hi.astype(f32)).astype(bf16)
    mixture = product(weights_hi, returned) + product(weights_lo, returned)
    output = hidden + residual_scale * mixture

    return (
        output.astype(bf16)[None],
        input_grad[None],
        gain_one_grad.reshape(-1),
        grad_query,
        grad_key,
        grad_value,
        grad_out,
        gain_two_grad.reshape(-1),
        grad_router,
        expert_sums[None, :shard_rows, :hidden_units],
        expert_sums[None, :shard_rows, hidden_units:],
        expert_sums[None, shard_rows:],
    )


def solution(mesh):
    fine = Mesh(mesh.devices.reshape(4, 4, 2, 2, 2), EVERY)
    rows, shards = P(("yl", "core"), CTX, None), P(("yl", "core"), None)
    gain, experts = P(("yl", "core")), P(CTX, ("yl", "core"), None)
    return jax.shard_map(
        on_device,
        mesh=fine,
        in_specs=(
            rows, rows, P(), gain, shards, shards, shards, shards, gain, shards, experts, experts, experts, rows,
        ),
        out_specs=(
            rows, rows, gain, shards, shards, shards, shards, gain, shards, experts, experts, experts,
        ),
        check_vma=False,
    )
```

profile of v0, /device:TPU:0, one launch (start us, length us, event | category | flops | bytes accessed | tf_op | source)
XLA Modules:
  0.0 528.4 jit_solution(5780565725787304933)
XLA Ops:
  6.8 1.4 shard_map.230
  8.3 8.2 %all-to-all-start = ((bf16[8,128,1024]{2,1,0:T(8,128)(2,1)}), bf16[8,128,1024]{2,1,0:T(8,128)(2,1)}, u32[]{:S(2)}, u32[]{:S(2)}) async-start(bf16[8,128,1024]{2,1,0:T(8,128)(2,1)} %shard_map.230), calls=%async_computation | async-start | bytes 4194304 | tf_op jit(solution)/shard_map/all_to_all | solution.py:58
  22.3 3.0 multiply_sine_fusion
  25.4 3.3 concatenate.33.cos_ref.refs_5_
  29.5 3.8 concatenate.35.sin_ref.refs_6_
  34.0 11.9 %collective-permute-done.1.refs_3_ = bf16[272,384]{1,0:T(8,128)(2,1)S(1)} collective-permute-done((bf16[272,384]{1,0:T(8,128)(2,1)S(1)}, bf16[272,384]{1,0:T(8,128)(2,1)S(1)}, u32[]{:S(2)}, u32[]{:S(2)}) %collective-permute-start.1) | collective-permute-done | bytes 208928 | tf_op jit(solution)/shard_map/ppermute | solution.py:71
  46.6 2.8 collective-permute-done.2.refs_4_
  53.7 4.5 shard_map.232
  60.3 1.5 collective-permute-start.3
  61.8 2.7 collective-permute-start.4
  64.5 1.4 collective-permute-start.5
  68.3 9.0 %collective-permute-done.7.refs_5_.refs_4_.refs_10_ = bf16[256,1024]{1,0:T(8,128)(2,1)S(1)} collective-permute-done((bf16[256,1024]{1,0:T(8,128)(2,1)}, bf16[256,1024]{1,0:T(8,128)(2,1)S(1)}, u32[]{:S(2)}, u32[]{:S(2)}) %collective-permute-start.7) | collective-permute-done | bytes 524320 | tf_op jit(solution)/shard_map/ppermute | solution.py:46
  77.4 2.9 shard_map.234
  80.3 11.0 %all-to-all-start.1 = ((bf16[32,48,1152]{2,1,0:T(8,128)(2,1)}), bf16[32,48,1152]{2,1,0:T(8,128)(2,1)}, u32[]{:S(2)}, u32[]{:S(2)}) async-start(bf16[32,48,1152]{2,1,0:T(8,128)(2,1)} %bitcast.126), calls=%async_computation.1 | async-start | bytes 7077888 | tf_op jit(solution)/shard_map/all_to_all | solution.py:58
  93.9 23.8 %shard_map.233 = (bf16[1024,128]{1,0:T(8,128)(2,1)S(1)}, f32[8,64,256]{2,1,0:T(8,128)S(1)}, f32[8,1,256]{2,1,0:T(1,128)S(1)}) custom-call(s32[16]{0:T(128)S(1)} %select_reduce_fusion.order_ref, s32[16]{0:T(128)S(1)} %lt.46.qnum_ref, s32[64]{0:T(128)S(1)} %reshape.234.knum_ref, bf16[1024,128]{1,0:T(8,128)(2,1)S(1)} %copy-done.58, ...), custom_call_target="tpu_custom_call" | custom-call | flops 12000000000 | bytes 4000000 | tf_op jit(solution)/shard_map/pallas_call | solution.py:587
  119.8 17.4 %all-to-all-done.1 = bf16[32,48,1152]{2,1,0:T(8,128)(2,1)} async-done(((bf16[32,48,1152]{2,1,0:T(8,128)(2,1)}), bf16[32,48,1152]{2,1,0:T(8,128)(2,1)}, u32[]{:S(2)}, u32[]{:S(2)}) %all-to-all-start.1) | async-done | bytes 3538976 | tf_op jit(solution)/shard_map/all_to_all | solution.py:58
  140.3 7.3 %all-to-all-start.2 = ((bf16[8,128,128]{2,1,0:T(8,128)(2,1)}), bf16[8,128,128]{2,1,0:T(8,128)(2,1)}, u32[]{:S(2)}, u32[]{:S(2)}) async-start(bf16[8,128,128]{2,1,0:T(8,128)(2,1)} %bitcast.123), calls=%async_computation.2 | async-start | bytes 524288 | tf_op jit(solution)/shard_map/all_to_all | solution.py:58
  147.7 8.9 %all-to-all-done.2.refs_1_ = bf16[8,128,128]{2,1,0:T(8,128)(2,1)} async-done(((bf16[8,128,128]{2,1,0:T(8,128)(2,1)}), bf16[8,128,128]{2,1,0:T(8,128)(2,1)}, u32[]{:S(2)}, u32[]{:S(2)}) %all-to-all-start.2) | async-done | bytes 262176 | tf_op jit(solution)/shard_map/all_to_all | solution.py:58
  157.4 4.7 shard_map.235
  164.9 5.0 all-to-all-start.3
  169.9 40.5 %all-to-all-done.3 = bf16[32,48,1024]{2,1,0:T(8,128)(2,1)} async-done(((bf16[32,48,1024]{2,1,0:T(8,128)(2,1)}), bf16[32,48,1024]{2,1,0:T(8,128)(2,1)}, u32[]{:S(2)}, u32[]{:S(2)}) %all-to-all-start.3) | async-done | bytes 3145760 | tf_op jit(solution)/shard_map/all_to_all | solution.py:58
  210.4 19.1 %shard_map.236 = (bf16[1536,1024]{1,0:T(8,128)(2,1)}, bf16[1536,1152]{1,0:T(8,128)(2,1)}, bf16[1536,1024]{1,0:T(8,128)(2,1)}, bf16[1536,512]{1,0:T(8,128)(2,1)}, bf16[1536,1024]{1,0:T(8,128)(2,1)}) custom-call(s32[1]{0:T(128)} %bitcast.23.expert_ref, s32[1]{0:T(128)} %bitcast.refs_0_.me_ref, bf16[1536,1024]{1,0:T(8,128)(2,1)} %bitcast.25.rows_ref, ...), custom_call_target="tpu_custom_call" | custom-call | flops 10000000000 | bytes 22000000 | tf_op jit(solution)/shard_map/pallas_call | solution.py:567
  229.5 7.7 %convolution_convert_fusion = bf16[1024,1024]{1,0:T(8,128)(2,1)} fusion(bf16[1536,1024]{1,0:T(8,128)(2,1)} %bitcast.25.rows_ref, bf16[1536,1024]{1,0:T(8,128)(2,1)} %get-tuple-element.70), kind=kOutput, calls=%fused_computation.8 | convolution fusion | flops 3222274048 | bytes 8388608 | tf_op jit(solution)/shard_map/dot_general | solution.py:42
  237.2 7.6 %all-to-all-start.4 = ((bf16[32,48,1152]{2,1,0:T(8,128)(2,1)}), bf16[32,48,1152]{2,1,0:T(8,128)(2,1)}, u32[]{:S(2)}, u32[]{:S(2)}) async-start(bf16[32,48,1152]{2,1,0:T(8,128)(2,1)} %bitcast.132), calls=%async_computation.4 | async-start | bytes 7077888 | tf_op jit(solution)/shard_map/all_to_all | solution.py:58
  244.8 4.3 convolution_convert_fusion.1
  254.0 1.4 pad_maximum_fusion
  257.5 2.0 collective-permute-start.15
  259.5 2.5 fusion
  263.3 46.1 %collective-permute-done.15.refs_15_.refs_4_ = bf16[256,2048]{1,0:T(8,128)(2,1)} collective-permute-done((bf16[256,2048]{1,0:T(8,128)(2,1)S(1)}, bf16[256,2048]{1,0:T(8,128)(2,1)}, u32[]{:S(2)}, u32[]{:S(2)}) %collective-permute-start.15) | collective-permute-done | bytes 1048608 | tf_op jit(solution)/shard_map/ppermute | solution.py:46
  310.6 2.3 copy.72
  314.1 11.1 %collective-permute-done.13 = bf16[384,1024]{1,0:T(8,128)(2,1)} collective-permute-done((bf16[384,1024]{1,0:T(8,128)(2,1)}, bf16[384,1024]{1,0:T(8,128)(2,1)}, u32[]{:S(2)}, u32[]{:S(2)}) %collective-permute-start.13) | collective-permute-done | bytes 786464 | tf_op jit(solution)/shard_map/ppermute | solution.py:46
  325.2 2.9 convert_add_fusion.1.refs_12_
  332.9 4.5 shard_map.237
  338.2 20.9 %all_to_all.120 = bf16[8,128,128]{2,1,0:T(8,128)(2,1)S(1)} all-to-all(bf16[8,128,128]{2,1,0:T(8,128)(2,1)S(1)} %get-tuple-element.73), channel_id=1, replica_groups=mesh['x'=4,'z'=4,'yh'=2,'yl'=2,'core'=2] {'z','yh'}, dimensions={0} | all-to-all | bytes 524288 | tf_op jit(solution)/shard_map/all_to_all | solution.py:58
  362.3 5.5 %all-to-all-start.6 = ((bf16[32,48,1024]{2,1,0:T(8,128)(2,1)}), bf16[32,48,1024]{2,1,0:T(8,128)(2,1)}, u32[]{:S(2)}, u32[]{:S(2)}) async-start(bf16[32,48,1024]{2,1,0:T(8,128)(2,1)} %bitcast.133), calls=%async_computation.6 | async-start | bytes 6291456 | tf_op jit(solution)/shard_map/all_to_all | solution.py:58
  372.0 22.4 %shard_map.238 = (f32[1024,128]{1,0:T(8,128)S(1)}, bf16[1024,128]{1,0:T(8,128)(2,1)S(1)}, bf16[1024,128]{1,0:T(8,128)(2,1)S(1)}, bf16[1024,128]{1,0:T(8,128)(2,1)S(1)}, bf16[1024,128]{1,0:T(8,128)(2,1)S(1)}) custom-call(s32[16]{0:T(128)S(1)} %copy-done.61, s32[16]{0:T(128)S(1)} %lt.46.qnum_ref, s32[64]{0:T(128)S(1)} %copy-done.56, ...), custom_call_target="tpu_custom_call" | custom-call | flops 30000001024 | bytes 6000000 | tf_op jit(solution)/shard_map/pallas_call | solution.py:605
  395.9 3.5 collective-permute-start.17
  399.7 1.4 collective-permute-start.19
  401.1 11.9 %collective-permute-done.17.refs_2_.refs_6_ = bf16[1024,128]{1,0:T(8,128)(2,1)S(1)} collective-permute-done((bf16[1024,128]{1,0:T(8,128)(2,1)S(1)}, bf16[1024,128]{1,0:T(8,128)(2,1)S(1)}, u32[]{:S(2)}, u32[]{:S(2)}) %collective-permute-start.17) | collective-permute-done | bytes 262176 | tf_op jit(solution)/shard_map/ppermute | solution.py:50
  412.9 5.3 %collective-permute-done.18.refs_3_.refs_7_ = bf16[1024,128]{1,0:T(8,128)(2,1)S(1)} collective-permute-done((bf16[1024,128]{1,0:T(8,128)(2,1)S(1)}, bf16[1024,128]{1,0:T(8,128)(2,1)S(1)}, u32[]{:S(2)}, u32[]{:S(2)}) %collective-permute-start.18) | collective-permute-done | bytes 262176 | tf_op jit(solution)/shard_map/ppermute | solution.py:50
  419.8 2.8 collective-permute-done.28
  431.6 3.5 all-to-all-start.7
  437.0 2.1 collective-permute-start.21
  439.1 8.8 %collective-permute-done.29 = bf16[256,1152]{1,0:T(8,128)(2,1)} collective-permute-done((bf16[256,1152]{1,0:T(8,128)(2,1)S(1)}, bf16[256,1152]{1,0:T(8,128)(2,1)}, u32[]{:S(2)}, u32[]{:S(2)}) %collective-permute-start.29) | collective-permute-done | bytes 589856 | tf_op jit(solution)/shard_map/ppermute | solution.py:46
  447.9 2.2 fusion.8
  450.1 5.6 %collective-permute-done.21 = bf16[256,256]{1,0:T(8,128)(2,1)S(1)} collective-permute-done((bf16[256,256]{1,0:T(8,128)(2,1)S(1)}, bf16[256,256]{1,0:T(8,128)(2,1)S(1)}, u32[]{:S(2)}, u32[]{:S(2)}) %collective-permute-start.21) | collective-permute-done | bytes 131104 | tf_op jit(solution)/shard_map/ppermute | solution.py:46
  459.3 6.8 %all-to-all-start.8 = ((bf16[32,8,1152]{2,1,0:T(8,128)(2,1)}), bf16[32,8,1152]{2,1,0:T(8,128)(2,1)}, u32[]{:S(2)}, u32[]{:S(2)}) async-start(bf16[32,8,1152]{2,1,0:T(8,128)(2,1)} %bitcast.56), calls=%async_computation.8 | async-start | bytes 1179648 | tf_op jit(solution)/shard_map/all_to_all | solution.py:58
  467.1 4.4 shard_map.240
  472.6 1.8 collective-permute-start.22
  474.8 1.7 collective-permute-start.27
  476.5 2.7 collective-permute-start.23
  485.3 1.9 collective-permute-start.35
  487.5 2.6 collective-permute-start.31
  490.1 2.0 collective-permute-done.30.refs_6_
  492.6 3.1 collective-permute-done.32.refs_8_
  495.6 1.5 shard_map.243
  497.1 6.1 %all-to-all-start.9 = ((bf16[8,96,1152]{2,1,0:T(8,128)(2,1)}), bf16[8,96,1152]{2,1,0:T(8,128)(2,1)S(1)}, u32[]{:S(2)}, u32[]{:S(2)}) async-start(bf16[8,96,1152]{2,1,0:T(8,128)(2,1)} %shard_map.243), calls=%async_computation.9 | async-start | bytes 3538944 | tf_op jit(solution)/shard_map/all_to_all | solution.py:58
  504.2 1.4 copy.73
  505.6 1.9 slice_bitcast_fusion
  507.5 2.2 slice_bitcast_fusion.1
  509.7 2.6 fusion.13
  512.3 3.3 fusion.9
  515.6 9.9 %all-to-all-done.9.refs_0_ = bf16[8,96,1152]{2,1,0:T(8,128)(2,1)S(1)} async-done(((bf16[8,96,1152]{2,1,0:T(8,128)(2,1)}), bf16[8,96,1152]{2,1,0:T(8,128)(2,1)S(1)}, u32[]{:S(2)}, u32[]{:S(2)}) %all-to-all-start.9) | async-done | bytes 1769504 | tf_op jit(solution)/shard_map/all_to_all | solution.py:58
  525.4 1.8 shard_map.244
  (281 shorter events, 82.3 us)
Async XLA Ops:
  8.3 10.1 %copy-start.71 = (bf16[1,128,1024]{2,1,0:T(8,128)(2,1)S(1)}, bf16[1,128,1024]{2,1,0:T(8,128)(2,1)}, u32[]{:S(2)}) copy-start(bf16[1,128,1024]{2,1,0:T(8,128)(2,1)} %param.26) | copy-start | bytes 786436
  8.3 10.1 %copy-start.72 = (bf16[1,256,512]{2,1,0:T(8,128)(2,1)S(1)}, bf16[1,256,512]{2,1,0:T(8,128)(2,1)}, u32[]{:S(2)}) copy-start(bf16[1,256,512]{2,1,0:T(8,128)(2,1)} %param.25) | copy-start | bytes 786436
  8.3 10.1 %copy-start.73 = (bf16[1,256,512]{2,1,0:T(8,128)(2,1)S(1)}, bf16[1,256,512]{2,1,0:T(8,128)(2,1)}, u32[]{:S(2)}) copy-start(bf16[1,256,512]{2,1,0:T(8,128)(2,1)} %param.24) | copy-start | bytes 786436
  8.3 13.1 %copy-start.78 = (s32[32]{0:T(128)S(1)}, s32[32]{0:T(128)}, u32[]{:S(2)}) copy-start(s32[32]{0:T(128)} %param.16) | copy-start | bytes 388
  8.3 45.4 %all-to-all-start = ((bf16[8,128,1024]{2,1,0:T(8,128)(2,1)}), bf16[8,128,1024]{2,1,0:T(8,128)(2,1)}, u32[]{:S(2)}, u32[]{:S(2)}) async-start(bf16[8,128,1024]{2,1,0:T(8,128)(2,1)} %shard_map.230), calls=%async_computation | async-start | bytes 4194304 | tf_op jit(solution)/shard_map/all_to_all | solution.py:58
  16.5 16.9 %collective-permute-start = (bf16[272,384]{1,0:T(8,128)(2,1)S(1)}, bf16[272,384]{1,0:T(8,128)(2,1)S(1)}, u32[]{:S(2)}, u32[]{:S(2)}) collective-permute-start(bf16[272,384]{1,0:T(8,128)(2,1)S(1)} %shard_map.229.refs_1_), channel_id=1, source_target_pairs={{0,1},{1,0},{2,3},{3,2},{4,5},{5,4},{6,7},{7,6},{8,9},{9,8},{10,11... | collective-permute-start | bytes 626696 | tf_op jit(solution)/shard_map/ppermute | solution.py:71
  16.5 29.5 %collective-permute-start.1 = (bf16[272,384]{1,0:T(8,128)(2,1)S(1)}, bf16[272,384]{1,0:T(8,128)(2,1)S(1)}, u32[]{:S(2)}, u32[]{:S(2)}) collective-permute-start(bf16[272,384]{1,0:T(8,128)(2,1)S(1)} %shard_map.229.refs_1_), channel_id=1, source_target_pairs={{0,2},{1,3},{2,0},{3,1},{4,6},{5,7},{6,4},{7,5},{8,10},{9,11},{10,... | collective-permute-start | bytes 626696 | tf_op jit(solution)/shard_map/ppermute | solution.py:71
  17.2 32.2 %collective-permute-start.2 = (bf16[272,384]{1,0:T(8,128)(2,1)S(1)}, bf16[272,384]{1,0:T(8,128)(2,1)S(1)}, u32[]{:S(2)}, u32[]{:S(2)}) collective-permute-start(bf16[272,384]{1,0:T(8,128)(2,1)S(1)} %shard_map.229.refs_1_), channel_id=1, source_target_pairs={{0,3},{1,2},{2,1},{3,0},{4,7},{5,6},{6,5},{7,4},{8,11},{9,10},{10,... | collective-permute-start | bytes 626696 | tf_op jit(solution)/shard_map/ppermute | solution.py:71
  19.3 58.1 %collective-permute-start.6 = (bf16[384,1024]{1,0:T(8,128)(2,1)}, bf16[384,1024]{1,0:T(8,128)(2,1)}, u32[]{:S(2)}, u32[]{:S(2)}) collective-permute-start(bf16[384,1024]{1,0:T(8,128)(2,1)} %pad_maximum_fusion.1.refs_11_.piece0), channel_id=1, source_target_pairs={{0,2},{2,0},{1,3},{3,1},{4,6},{6,4},{5,7},{7,5},{8,10},{10,8},{9,1... | collective-permute-start | bytes 2359304 | tf_op jit(solution)/shard_map/ppermute | solution.py:46
  20.0 57.4 %collective-permute-start.7 = (bf16[256,1024]{1,0:T(8,128)(2,1)}, bf16[256,1024]{1,0:T(8,128)(2,1)S(1)}, u32[]{:S(2)}, u32[]{:S(2)}) collective-permute-start(bf16[256,1024]{1,0:T(8,128)(2,1)} %refs_8_.1), channel_id=1, source_target_pairs={{0,2},{2,0},{1,3},{3,1},{4,6},{6,4},{5,7},{7,5},{8,10},{10,8},{9,1... | collective-permute-start | bytes 1572872 | tf_op jit(solution)/shard_map/ppermute | solution.py:46
  60.3 17.1 %collective-permute-start.3 = (bf16[1024,128]{1,0:T(8,128)(2,1)}, bf16[1024,128]{1,0:T(8,128)(2,1)}, u32[]{:S(2)}, u32[]{:S(2)}) collective-permute-start(bf16[1024,128]{1,0:T(8,128)(2,1)} %get-tuple-element.61.kv0), channel_id=1, source_target_pairs={{0,32},{32,64},{64,96},{96,0},{1,33},{33,65},{65,97},{97,1},{2,34}... | collective-permute-start | bytes 786440 | tf_op jit(solution)/shard_map/ppermute | solution.py:50
  61.8 15.6 %collective-permute-start.4 = (bf16[1024,128]{1,0:T(8,128)(2,1)}, bf16[1024,128]{1,0:T(8,128)(2,1)}, u32[]{:S(2)}, u32[]{:S(2)}) collective-permute-start(bf16[1024,128]{1,0:T(8,128)(2,1)} %get-tuple-element.61.kv0), channel_id=1, source_target_pairs={{0,64},{32,96},{64,0},{96,32},{1,65},{33,97},{65,1},{97,33},{2,66}... | collective-permute-start | bytes 786440 | tf_op jit(solution)/shard_map/ppermute | solution.py:50
  64.5 12.9 %collective-permute-start.5 = (bf16[1024,128]{1,0:T(8,128)(2,1)}, bf16[1024,128]{1,0:T(8,128)(2,1)}, u32[]{:S(2)}, u32[]{:S(2)}) collective-permute-start(bf16[1024,128]{1,0:T(8,128)(2,1)} %get-tuple-element.61.kv0), channel_id=1, source_target_pairs={{0,96},{32,0},{64,32},{96,64},{1,97},{33,1},{65,33},{97,65},{2,98}... | collective-permute-start | bytes 786440 | tf_op jit(solution)/shard_map/ppermute | solution.py:50
  77.4 79.2 %copy-start.1 = (bf16[256,1024]{1,0:T(8,128)(2,1)}, bf16[256,1024]{1,0:T(8,128)(2,1)S(1)}, u32[]{:S(2)}) copy-start(bf16[256,1024]{1,0:T(8,128)(2,1)S(1)} %collective-permute-done.7.refs_5_.refs_4_.refs_10_) | copy-start | bytes 1572868
  80.3 56.9 %all-to-all-start.1 = ((bf16[32,48,1152]{2,1,0:T(8,128)(2,1)}), bf16[32,48,1152]{2,1,0:T(8,128)(2,1)}, u32[]{:S(2)}, u32[]{:S(2)}) async-start(bf16[32,48,1152]{2,1,0:T(8,128)(2,1)} %bitcast.126), calls=%async_computation.1 | async-start | bytes 7077888 | tf_op jit(solution)/shard_map/all_to_all | solution.py:58
  91.3 56.4 %collective-permute-start.10 = (bf16[384,1024]{1,0:T(8,128)(2,1)}, bf16[384,1024]{1,0:T(8,128)(2,1)}, u32[]{:S(2)}, u32[]{:S(2)}) collective-permute-start(bf16[384,1024]{1,0:T(8,128)(2,1)} %pad_maximum_fusion.1.refs_11_.piece0), channel_id=1, source_target_pairs={{0,1},{1,0},{2,3},{3,2},{4,5},{5,4},{6,7},{7,6},{8,9},{9,8},{10,11... | collective-permute-start | bytes 2359304 | tf_op jit(solution)/shard_map/ppermute | solution.py:46
  91.4 56.3 %collective-permute-start.8 = (bf16[256,1024]{1,0:T(8,128)(2,1)}, bf16[256,1024]{1,0:T(8,128)(2,1)}, u32[]{:S(2)}, u32[]{:S(2)}) collective-permute-start(bf16[256,1024]{1,0:T(8,128)(2,1)} %refs_8_.1), channel_id=1, source_target_pairs={{0,1},{1,0},{2,3},{3,2},{4,5},{5,4},{6,7},{7,6},{8,9},{9,8},{10,11... | collective-permute-start | bytes 1572872 | tf_op jit(solution)/shard_map/ppermute | solution.py:46
  92.1 25.6 %copy-start.55 = (s32[64]{0:T(128)}, s32[64]{0:T(128)S(1)}, u32[]{:S(2)}) copy-start(s32[64]{0:T(128)S(1)} %reshape.234.knum_ref) | copy-start | bytes 772
  92.4 55.3 %collective-permute-start.9 = (bf16[256,1024]{1,0:T(8,128)(2,1)S(1)}, bf16[256,1024]{1,0:T(8,128)(2,1)}, u32[]{:S(2)}, u32[]{:S(2)}) collective-permute-start(bf16[256,1024]{1,0:T(8,128)(2,1)S(1)} %collective-permute-done.7.refs_5_.refs_4_.refs_10_), channel_id=1, source_target_pairs={{0,1},{1,0},{2,3},{3,2},{4,5},{5,4},{6,7},{7,6},{8,9},{9,8},{10,11... | collective-permute-start | bytes 1572872 | tf_op jit(solution)/shard_map/ppermute | solution.py:46
  92.6 55.1 %collective-permute-start.11 = (bf16[384,1024]{1,0:T(8,128)(2,1)}, bf16[384,1024]{1,0:T(8,128)(2,1)}, u32[]{:S(2)}, u32[]{:S(2)}) collective-permute-start(bf16[384,1024]{1,0:T(8,128)(2,1)} %collective-permute-done.6.held_ref.refs_6_.refs_13_.piece2), channel_id=1, source_target_pairs={{0,1},{1,0},{2,3},{3,2},{4,5},{5,4},{6,7},{7,6},{8,9},{9,8},{10,11... | collective-permute-start | bytes 2359304 | tf_op jit(solution)/shard_map/ppermute | solution.py:46
  93.9 62.6 %copy-start.4 = (bf16[1,128,1024]{2,1,0:T(8,128)(2,1)S(1)}, bf16[1,128,1024]{2,1,0:T(8,128)(2,1)}, u32[]{:S(2)}) copy-start(bf16[1,128,1024]{2,1,0:T(8,128)(2,1)} %param.14) | copy-start | bytes 786436
  93.9 62.6 %copy-start.14 = (bf16[1024,32]{1,0:T(8,128)(2,1)S(1)}, bf16[1024,32]{1,0:T(8,128)(2,1)}, u32[]{:S(2)}) copy-start(bf16[1024,32]{1,0:T(8,128)(2,1)} %copy-done.13) | copy-start | bytes 196612
  140.3 16.2 %all-to-all-start.2 = ((bf16[8,128,128]{2,1,0:T(8,128)(2,1)}), bf16[8,128,128]{2,1,0:T(8,128)(2,1)}, u32[]{:S(2)}, u32[]{:S(2)}) async-start(bf16[8,128,128]{2,1,0:T(8,128)(2,1)} %bitcast.123), calls=%async_computation.2 | async-start | bytes 524288 | tf_op jit(solution)/shard_map/all_to_all | solution.py:58
  164.9 45.5 %all-to-all-start.3 = ((bf16[32,48,1024]{2,1,0:T(8,128)(2,1)}), bf16[32,48,1024]{2,1,0:T(8,128)(2,1)}, u32[]{:S(2)}, u32[]{:S(2)}) async-start(bf16[32,48,1024]{2,1,0:T(8,128)(2,1)} %bitcast.134), calls=%async_computation.3 | async-start | bytes 6291456 | tf_op jit(solution)/shard_map/all_to_all | solution.py:58
  237.2 90.9 %all-to-all-start.4 = ((bf16[32,48,1152]{2,1,0:T(8,128)(2,1)}), bf16[32,48,1152]{2,1,0:T(8,128)(2,1)}, u32[]{:S(2)}, u32[]{:S(2)}) async-start(bf16[32,48,1152]{2,1,0:T(8,128)(2,1)} %bitcast.132), calls=%async_computation.4 | async-start | bytes 7077888 | tf_op jit(solution)/shard_map/all_to_all | solution.py:58
  250.6 8.9 %collective-permute-start.12 = (bf16[2,384,1024]{2,1,0:T(8,128)(2,1)}, bf16[2,384,1024]{2,1,0:T(8,128)(2,1)}, u32[]{:S(2)}, u32[]{:S(2)}) collective-permute-start(bf16[2,384,1024]{2,1,0:T(8,128)(2,1)} %fusion.2), channel_id=1, source_target_pairs={{0,1},{1,0},{2,3},{3,2},{4,5},{5,4},{6,7},{7,6},{8,9},{9,8},{10,11... | collective-permute-start | bytes 4718600 | tf_op jit(solution)/shard_map/ppermute | solution.py:46
  257.5 51.9 %collective-permute-start.15 = (bf16[256,2048]{1,0:T(8,128)(2,1)S(1)}, bf16[256,2048]{1,0:T(8,128)(2,1)}, u32[]{:S(2)}, u32[]{:S(2)}) collective-permute-start(bf16[256,2048]{1,0:T(8,128)(2,1)S(1)} %constant_dynamic-update-slice_fusion.3.refs_13_.refs_2_), channel_id=1, source_target_pairs={{0,2},{2,0},{1,3},{3,1},{4,6},{6,4},{5,7},{7,5},{8,10},{10,8},{9,1... | collective-permute-start | bytes 3145736 | tf_op jit(solution)/shard_map/ppermute | solution.py:46
  259.5 50.2 %copy-start.76 = (s32[128,32]{0,1:T(8,128)S(1)}, s32[128,32]{0,1:T(8,128)}, u32[]{:S(2)}) copy-start(s32[128,32]{0,1:T(8,128)} %copy-done.75) | copy-start | bytes 49156
  262.0 47.4 %copy-start.67 = (bf16[2,384,1024]{2,1,0:T(8,128)(2,1)}, bf16[2,384,1024]{2,1,0:T(8,128)(2,1)S(1)}, u32[]{:S(2)}) copy-start(bf16[2,384,1024]{2,1,0:T(8,128)(2,1)S(1)} %fusion) | copy-start | bytes 4718596
  263.1 62.1 %collective-permute-start.13 = (bf16[384,1024]{1,0:T(8,128)(2,1)}, bf16[384,1024]{1,0:T(8,128)(2,1)}, u32[]{:S(2)}, u32[]{:S(2)}) collective-permute-start(bf16[384,1024]{1,0:T(8,128)(2,1)} %dynamic-slice_bitcast_fusion), channel_id=1, source_target_pairs={{0,2},{2,0},{1,3},{3,1},{4,6},{6,4},{5,7},{7,5},{8,10},{10,8},{9,1... | collective-permute-start | bytes 2359304 | tf_op jit(solution)/shard_map/ppermute | solution.py:46
  263.3 64.8 %collective-permute-start.14 = (bf16[256,2048]{1,0:T(8,128)(2,1)S(1)}, bf16[256,2048]{1,0:T(8,128)(2,1)}, u32[]{:S(2)}, u32[]{:S(2)}) collective-permute-start(bf16[256,2048]{1,0:T(8,128)(2,1)S(1)} %constant_dynamic-update-slice_fusion.3.refs_13_.refs_2_), channel_id=1, source_target_pairs={{0,1},{1,0},{2,3},{3,2},{4,5},{5,4},{6,7},{7,6},{8,9},{9,8},{10,11... | collective-permute-start | bytes 3145736 | tf_op jit(solution)/shard_map/ppermute | solution.py:46
  309.4 18.7 %collective-permute-start.16 = (bf16[256,2048]{1,0:T(8,128)(2,1)}, bf16[256,2048]{1,0:T(8,128)(2,1)}, u32[]{:S(2)}, u32[]{:S(2)}) collective-permute-start(bf16[256,2048]{1,0:T(8,128)(2,1)} %collective-permute-done.15.refs_15_.refs_4_), channel_id=1, source_target_pairs={{0,1},{1,0},{2,3},{3,2},{4,5},{5,4},{6,7},{7,6},{8,9},{9,8},{10,11... | collective-permute-start | bytes 3145736 | tf_op jit(solution)/shard_map/ppermute | solution.py:46
  338.2 21.4 %copy-start.45 = (bf16[128,1024]{1,0:T(8,128)(2,1)}, bf16[128,1024]{1,0:T(8,128)(2,1)S(1)}, u32[]{:S(2)}) copy-start(bf16[128,1024]{1,0:T(8,128)(2,1)S(1)} %get-tuple-element.91.refs_2_) | copy-start | bytes 786436
  338.2 22.8 %copy-start.53 = (bf16[128,32]{1,0:T(8,128)(2,1)}, bf16[128,32]{1,0:T(8,128)(2,1)S(1)}, u32[]{:S(2)}) copy-start(bf16[128,32]{1,0:T(8,128)(2,1)S(1)} %get-tuple-element.93.refs_4_) | copy-start | bytes 24580
  362.3 5.5 %copy-start.56 = (s32[64]{0:T(128)S(1)}, s32[64]{0:T(128)}, u32[]{:S(2)}) copy-start(s32[64]{0:T(128)} %copy-done.55) | copy-start | bytes 772
  362.3 61.7 %all-to-all-start.6 = ((bf16[32,48,1024]{2,1,0:T(8,128)(2,1)}), bf16[32,48,1024]{2,1,0:T(8,128)(2,1)}, u32[]{:S(2)}, u32[]{:S(2)}) async-start(bf16[32,48,1024]{2,1,0:T(8,128)(2,1)} %bitcast.133), calls=%async_computation.6 | async-start | bytes 6291456 | tf_op jit(solution)/shard_map/all_to_all | solution.py:58
  372.0 46.2 %copy-start.42 = (bf16[128,1024]{1,0:T(8,128)(2,1)S(1)}, bf16[128,1024]{1,0:T(8,128)(2,1)}, u32[]{:S(2)}) copy-start(bf16[128,1024]{1,0:T(8,128)(2,1)} %copy-done.41) | copy-start | bytes 786436
  372.0 46.2 %copy-start.44 = (bf16[128,1024]{1,0:T(8,128)(2,1)S(1)}, bf16[128,1024]{1,0:T(8,128)(2,1)}, u32[]{:S(2)}) copy-start(bf16[128,1024]{1,0:T(8,128)(2,1)} %copy-done.43) | copy-start | bytes 786436
  372.0 46.2 %copy-start.46 = (bf16[128,1024]{1,0:T(8,128)(2,1)S(1)}, bf16[128,1024]{1,0:T(8,128)(2,1)}, u32[]{:S(2)}) copy-start(bf16[128,1024]{1,0:T(8,128)(2,1)} %copy-done.45) | copy-start | bytes 786436
  372.0 46.3 %copy-start.54 = (bf16[128,32]{1,0:T(8,128)(2,1)S(1)}, bf16[128,32]{1,0:T(8,128)(2,1)}, u32[]{:S(2)}) copy-start(bf16[128,32]{1,0:T(8,128)(2,1)} %copy-done.53) | copy-start | bytes 24580
  395.9 17.0 %collective-permute-start.17 = (bf16[1024,128]{1,0:T(8,128)(2,1)S(1)}, bf16[1024,128]{1,0:T(8,128)(2,1)S(1)}, u32[]{:S(2)}, u32[]{:S(2)}) collective-permute-start(bf16[1024,128]{1,0:T(8,128)(2,1)S(1)} %get-tuple-element.78), channel_id=1, source_target_pairs={{0,96},{32,0},{64,32},{96,64},{1,97},{33,1},{65,33},{97,65},{2,98}... | collective-permute-start | bytes 786440 | tf_op jit(solution)/shard_map/ppermute | solution.py:50
  399.4 18.8 %collective-permute-start.18 = (bf16[1024,128]{1,0:T(8,128)(2,1)S(1)}, bf16[1024,128]{1,0:T(8,128)(2,1)S(1)}, u32[]{:S(2)}, u32[]{:S(2)}) collective-permute-start(bf16[1024,128]{1,0:T(8,128)(2,1)S(1)} %get-tuple-element.79), channel_id=1, source_target_pairs={{0,64},{32,96},{64,0},{96,32},{1,65},{33,97},{65,1},{97,33},{2,66}... | collective-permute-start | bytes 786440 | tf_op jit(solution)/shard_map/ppermute | solution.py:50
  399.7 18.5 %collective-permute-start.19 = (bf16[1024,128]{1,0:T(8,128)(2,1)S(1)}, bf16[1024,128]{1,0:T(8,128)(2,1)S(1)}, u32[]{:S(2)}, u32[]{:S(2)}) collective-permute-start(bf16[1024,128]{1,0:T(8,128)(2,1)S(1)} %get-tuple-element.80), channel_id=1, source_target_pairs={{0,32},{32,64},{64,96},{96,0},{1,33},{33,65},{65,97},{97,1},{2,34}... | collective-permute-start | bytes 786440 | tf_op jit(solution)/shard_map/ppermute | solution.py:50
  419.8 2.8 collective-permute-start.28
  431.3 3.9 collective-permute-start.20
  431.5 16.3 %collective-permute-start.29 = (bf16[256,1152]{1,0:T(8,128)(2,1)S(1)}, bf16[256,1152]{1,0:T(8,128)(2,1)}, u32[]{:S(2)}, u32[]{:S(2)}) collective-permute-start(bf16[256,1152]{1,0:T(8,128)(2,1)S(1)} %dynamic-slice_bitcast_fusion.1), channel_id=1, source_target_pairs={{0,2},{2,0},{1,3},{3,1},{4,6},{6,4},{5,7},{7,5},{8,10},{10,8},{9,1... | collective-permute-start | bytes 1769480 | tf_op jit(solution)/shard_map/ppermute | solution.py:46
  431.6 24.6 %all-to-all-start.7 = ((bf16[8,128,256]{2,1,0:T(8,128)(2,1)}), bf16[8,128,256]{2,1,0:T(8,128)(2,1)S(1)}, u32[]{:S(2)}, u32[]{:S(2)}) async-start(bf16[8,128,256]{2,1,0:T(8,128)(2,1)} %bitcast.115), calls=%async_computation.7 | async-start | bytes 1048576 | tf_op jit(solution)/shard_map/all_to_all | solution.py:58
  435.9 30.2 %copy-start.5 = (bf16[1,128,1024]{2,1,0:T(8,128)(2,1)S(1)}, bf16[1,128,1024]{2,1,0:T(8,128)(2,1)}, u32[]{:S(2)}) copy-start(bf16[1,128,1024]{2,1,0:T(8,128)(2,1)} %param.14) | copy-start | bytes 786436
  437.0 18.7 %collective-permute-start.21 = (bf16[256,256]{1,0:T(8,128)(2,1)S(1)}, bf16[256,256]{1,0:T(8,128)(2,1)S(1)}, u32[]{:S(2)}, u32[]{:S(2)}) collective-permute-start(bf16[256,256]{1,0:T(8,128)(2,1)S(1)} %dynamic-slice_bitcast_fusion.2), channel_id=1, source_target_pairs={{0,2},{2,0},{1,3},{3,1},{4,6},{6,4},{5,7},{7,5},{8,10},{10,8},{9,1... | collective-permute-start | bytes 393224 | tf_op jit(solution)/shard_map/ppermute | solution.py:46
  459.3 20.7 %all-to-all-start.8 = ((bf16[32,8,1152]{2,1,0:T(8,128)(2,1)}), bf16[32,8,1152]{2,1,0:T(8,128)(2,1)}, u32[]{:S(2)}, u32[]{:S(2)}) async-start(bf16[32,8,1152]{2,1,0:T(8,128)(2,1)} %bitcast.56), calls=%async_computation.8 | async-start | bytes 1179648 | tf_op jit(solution)/shard_map/all_to_all | solution.py:58
  472.6 12.7 %collective-permute-start.22 = (bf16[256,256]{1,0:T(8,128)(2,1)S(1)}, bf16[256,256]{1,0:T(8,128)(2,1)S(1)}, u32[]{:S(2)}, u32[]{:S(2)}) collective-permute-start(bf16[256,256]{1,0:T(8,128)(2,1)S(1)} %constant_dynamic-update-slice_fusion.1.refs_1_), channel_id=1, source_target_pairs={{0,32},{32,64},{64,96},{96,0},{1,33},{33,65},{65,97},{97,1},{2,34}... | collective-permute-start | bytes 393224 | tf_op jit(solution)/shard_map/ppermute | solution.py:50
  474.4 7.9 %collective-permute-start.25 = (f32[1,256]{1,0:T(1,128)S(1)}, f32[1,256]{1,0:T(1,128)S(1)}, u32[]{:S(2)}, u32[]{:S(2)}) collective-permute-start(f32[1,256]{1,0:T(1,128)S(1)} %get-tuple-element.87), channel_id=1, source_target_pairs={{0,1},{1,0},{2,3},{3,2},{4,5},{5,4},{6,7},{7,6},{8,9},{9,8},{10,11... | collective-permute-start | bytes 3080 | tf_op jit(solution)/shard_map/ppermute | solution.py:821
  474.5 8.8 %collective-permute-start.26 = (f32[1,256]{1,0:T(1,128)S(1)}, f32[1,256]{1,0:T(1,128)S(1)}, u32[]{:S(2)}, u32[]{:S(2)}) collective-permute-start(f32[1,256]{1,0:T(1,128)S(1)} %get-tuple-element.88), channel_id=1, source_target_pairs={{0,2},{1,3},{2,0},{3,1},{4,6},{5,7},{6,4},{7,5},{8,10},{9,11},{10,... | collective-permute-start | bytes 3080 | tf_op jit(solution)/shard_map/ppermute | solution.py:821
  474.8 9.6 %collective-permute-start.27 = (f32[1,256]{1,0:T(1,128)S(1)}, f32[1,256]{1,0:T(1,128)S(1)}, u32[]{:S(2)}, u32[]{:S(2)}) collective-permute-start(f32[1,256]{1,0:T(1,128)S(1)} %get-tuple-element.89), channel_id=1, source_target_pairs={{0,3},{1,2},{2,1},{3,0},{4,7},{5,6},{6,5},{7,4},{8,11},{9,10},{10,... | collective-permute-start | bytes 3080 | tf_op jit(solution)/shard_map/ppermute | solution.py:821
  476.5 10.7 %collective-permute-start.23 = (bf16[256,256]{1,0:T(8,128)(2,1)S(1)}, bf16[256,256]{1,0:T(8,128)(2,1)S(1)}, u32[]{:S(2)}, u32[]{:S(2)}) collective-permute-start(bf16[256,256]{1,0:T(8,128)(2,1)S(1)} %constant_dynamic-update-slice_fusion.1.refs_1_), channel_id=1, source_target_pairs={{0,64},{32,96},{64,0},{96,32},{1,65},{33,97},{65,1},{97,33},{2,66}... | collective-permute-start | bytes 393224 | tf_op jit(solution)/shard_map/ppermute | solution.py:50
  482.3 5.2 collective-permute-start.24
  483.2 12.4 %collective-permute-start.33 = (bf16[8,1152]{1,0:T(8,128)(2,1)S(1)}, bf16[8,1152]{1,0:T(8,128)(2,1)S(1)}, u32[]{:S(2)}, u32[]{:S(2)}) collective-permute-start(bf16[8,1152]{1,0:T(8,128)(2,1)S(1)} %reduce_sum.42.refs_9_), channel_id=1, source_target_pairs={{0,32},{32,64},{64,96},{96,0},{1,33},{33,65},{65,97},{97,1},{2,34}... | collective-permute-start | bytes 55304 | tf_op jit(solution)/shard_map/ppermute | solution.py:50
  484.4 11.2 %collective-permute-start.34 = (bf16[8,1152]{1,0:T(8,128)(2,1)S(1)}, bf16[8,1152]{1,0:T(8,128)(2,1)S(1)}, u32[]{:S(2)}, u32[]{:S(2)}) collective-permute-start(bf16[8,1152]{1,0:T(8,128)(2,1)S(1)} %reduce_sum.42.refs_9_), channel_id=1, source_target_pairs={{0,64},{32,96},{64,0},{96,32},{1,65},{33,97},{65,1},{97,33},{2,66}... | collective-permute-start | bytes 55304 | tf_op jit(solution)/shard_map/ppermute | solution.py:50
  485.3 10.3 %collective-permute-start.35 = (bf16[8,1152]{1,0:T(8,128)(2,1)S(1)}, bf16[8,1152]{1,0:T(8,128)(2,1)S(1)}, u32[]{:S(2)}, u32[]{:S(2)}) collective-permute-start(bf16[8,1152]{1,0:T(8,128)(2,1)S(1)} %reduce_sum.42.refs_9_), channel_id=1, source_target_pairs={{0,96},{32,0},{64,32},{96,64},{1,97},{33,1},{65,33},{97,65},{2,98}... | collective-permute-start | bytes 55304 | tf_op jit(solution)/shard_map/ppermute | solution.py:50
  487.2 4.8 collective-permute-start.30
  487.5 5.1 collective-permute-start.31
  492.0 3.6 collective-permute-start.32
  497.1 6.1 %copy-start.36 = (f32[128,32]{1,0:T(8,128)S(1)}, f32[128,32]{1,0:T(8,128)}, u32[]{:S(2)}) copy-start(f32[128,32]{1,0:T(8,128)} %copy-done.34) | copy-start | bytes 49156
  497.1 28.3 %all-to-all-start.9 = ((bf16[8,96,1152]{2,1,0:T(8,128)(2,1)}), bf16[8,96,1152]{2,1,0:T(8,128)(2,1)S(1)}, u32[]{:S(2)}, u32[]{:S(2)}) async-start(bf16[8,96,1152]{2,1,0:T(8,128)(2,1)} %shard_map.243), calls=%async_computation.9 | async-start | bytes 3538944 | tf_op jit(solution)/shard_map/all_to_all | solution.py:58
  (60 other events, 67.5 us)
where the time goes:
time: 539 us; the launch traced here: 528 us
  waiting for transfers between devices  198 us (37%)
  starting transfers between devices  95.9 us (18%)
  Pallas kernels  93.4 us (17%)
  local copies, waits for them, and re-layouts  71.7 us (13%)
  other arithmetic  23.6 us (4%)
  blocking collectives  20.9 us (4%)
  matrix products  18.1 us (3%)
  between operations  6.45 us (1%)
    ppermute x15, waiting for transfers between devices, swap(): return lax.ppermute(values, axis, [(0, 1), (1, 0)])  83.5 us
    all_to_all x9, waiting for transfers between devices, exchange(): lax.all_to_all(rows_first(values), axes, 0, 0, tiled=True)  77.4 us
    all_to_all x9, starting transfers between devices, exchange(): lax.all_to_all(rows_first(values), axes, 0, 0, tiled=True)  60.8 us
    unnamed x164, local copies, waits for them, and re-layouts  42.1 us
    pallas_call x1, Pallas kernels, attend(): pl.pallas_call(attend_kernel, out_shape=(jax.ShapeDtypeStruct((rows, 2 *...  23.8 us
    pallas_call x12, Pallas kernels, call(): pl.pallas_call(body, out_shape=tuple((jax.ShapeDtypeStruct(shape, dtype)...  23.7 us
    ppermute x15, starting transfers between devices, turn(): return lax.ppermute(values, axis, [(i, (i + step) % 4) for i in range(4)])  23.1 us
    ppermute x15, waiting for transfers between devices, turn(): return lax.ppermute(values, axis, [(i, (i + step) % 4) for i in range(4)])  22.7 us
  transfers between devices with their start and end apart: 45, of which 19 were waited for; matrix products, arithmetic and copies ran while one was open for 11% of the time, Pallas kernels for 11%

commit v1 on v0

--- a/solution.py
+++ b/solution.py
@@ -185,9 +185,8 @@
 
 
 def attend_kernel(
-    order_ref, qnum_ref, knum_ref, q_ref, kv0, kv1, kv2, kv3, held_ref, out_ref, turned_ref, lse_ref, kvs, kvt
-):
-    del held_ref
+    order_ref, qnum_ref, knum_ref, q_ref, kv0, kv1, kv2, kv3, out_ref, turned_ref, lse_ref, kvs, kvt
+):
     sort_keys(knum_ref, (kv0, kv1, kv2, kv3), kvs, kvt)
     width = 4 * HALF
 
@@ -367,31 +366,37 @@
         copies_ref[copy] = x_ref[...]
 
 
-def shard_kernel(head_ref, query_ref, key_ref, value_ref, router_ref, gain1_ref, gain2_ref, out_ref):
+def shard_kernel(
+    head_ref, query_ref, key_ref, value_ref, router_ref, gain1_ref, gain2_ref, out_ref, by_head_ref
+):
     rows = query_ref.shape[0]
-    head = head_ref[0]
-    out_ref[...] = jnp.zeros_like(out_ref)
-    out_ref[:rows, : 2 * HEAD_DIM] = query_ref[:, pl.ds(pl.multiple_of(head * 128, 128), 128)]
-    pair = pl.ds(pl.multiple_of((head // 2) * 128, 128), 128)
-    odd = jnp.full((rows, 128), head % 2, jnp.int32) == 1
-    column = lax.broadcasted_iota(jnp.int32, (rows, 128), 1)
-    keys, values = key_ref[:, pair].astype(f32), value_ref[:, pair].astype(f32)
-    keys = jnp.where(odd, pltpu.roll(keys, HEAD_DIM, 1), keys)
-    values = jnp.where(odd, values, pltpu.roll(values, HEAD_DIM, 1))
-    out_ref[:rows, 2 * HEAD_DIM : 4 * HEAD_DIM] = jnp.where(column < HEAD_DIM, keys, values).astype(bf16)
-    out_ref[:rows, 4 * HEAD_DIM : 4 * HEAD_DIM + EXPERTS] = router_ref[...]
+    lower = lax.broadcasted_iota(jnp.int32, (rows, 128), 1) < HEAD_DIM
+    for head in range(KV_HEADS):
+        pair = slice(head // 2 * 128, (head // 2 + 1) * 128)
+        keys, values = key_ref[:, pair].astype(f32), value_ref[:, pair].astype(f32)
+        if head % 2:
+            keys = pltpu.roll(keys, HEAD_DIM, 1)
+        else:
+            values = pltpu.roll(values, HEAD_DIM, 1)
+        by_head_ref[:, head * 256 : head * 256 + 128] = query_ref[:, head * 128 : (head + 1) * 128]
+        by_head_ref[:, head * 256 + 128 : (head + 1) * 256] = jnp.where(lower, keys, values).astype(bf16)
+    out_ref[:rows, :] = by_head_ref[:, pl.ds(pl.multiple_of(head_ref[0] * 256, 256), 256)]
+    router = jnp.concatenate([router_ref[...].astype(f32), jnp.zeros((rows, 128 - EXPERTS), f32)], axis=1)
+    out_ref[rows : rows + EXPERTS, :] = router.T[:EXPERTS].astype(bf16)
     row = lax.broadcasted_iota(jnp.int32, (16, rows), 0)
     gains = jnp.where(row == 0, gain1_ref[...].astype(f32), jnp.where(row == 1, gain2_ref[...].astype(f32), 0.0))
-    out_ref[rows:, :rows] = gains.astype(bf16)
+    out_ref[rows + EXPERTS :, :] = gains.astype(bf16)
 
 
 def small_kernel(me_ref, piece0, piece1, piece2, piece3, head_w_ref, router_ref, gain1_ref, gain2_ref):
     rows = head_w_ref.shape[0] // 4
     for step, piece in enumerate((piece0, piece1, piece2, piece3)):
         place = part_of(me_ref, step, rows)
-        head_w_ref[place, :] = piece[:rows, : 4 * HEAD_DIM]
-        router_ref[place, :] = piece[:rows, 4 * HEAD_DIM : 4 * HEAD_DIM + EXPERTS]
-        gains = piece[rows:, :rows].astype(f32)
+        head_w_ref[place, :] = piece[:rows, :]
+        router = piece[rows : rows + EXPERTS, :].astype(f32)
+        router = jnp.concatenate([router, jnp.zeros((128 - EXPERTS, rows), f32)], axis=0)
+        router_ref[place, :] = router.T[:, :EXPERTS].astype(bf16)
+        gains = piece[rows + EXPERTS :, :].astype(f32)
         gain1_ref[:, place] = gains[0:1]
         gain2_ref[:, place] = gains[1:2]
 
@@ -458,6 +463,17 @@
             router_grad = product_tn(normed_ref[:, columns], logit_grad)
             gain_grad = jnp.broadcast_to(gain_ref[:, columns], (128, part)).T
             ref[row, :, width:] = jnp.where(column == EXPERTS, gain_grad, router_grad).astype(bf16)
+
+
+def expert_grad_kernel(core_ref, rows_ref, pre_grad_ref, inner_ref, route_grad_ref, keep_ref, away_ref):
+    part = rows_ref.shape[1] // 4
+    for row in range(2):
+        for ref, core in ((keep_ref, core_ref[0]), (away_ref, 1 - core_ref[0])):
+            place = 2 * row + core
+            columns = pl.ds(pl.multiple_of(place * part, part), part)
+            ref[row, :part, :] = product_tn(rows_ref[:, columns], pre_grad_ref[...]).astype(bf16)
+            columns = pl.ds(pl.multiple_of(place * (part // 2), part // 2), part // 2)
+            ref[row, part:, :] = product_tn(inner_ref[:, columns], route_grad_ref[...]).astype(bf16)
 
 
 def head_grad_kernel(dq_ref, dkv0, dkv1, dkv2, dkv3, cos_ref, sin_ref, out_ref):
@@ -580,7 +596,7 @@
 VMEM = pl.BlockSpec(memory_space=pltpu.VMEM)
 
 
-def attend(numbers, queries, kv_parts, held):
+def attend(numbers, queries, kv_parts):
     rows = queries.shape[0]
     keys = rows * len(kv_parts)
     pairs = rows // (2 * HALF)
@@ -591,12 +607,12 @@
             jax.ShapeDtypeStruct((pairs, HEAD_DIM, 4 * HALF), f32),
             jax.ShapeDtypeStruct((pairs, 1, 4 * HALF), f32),
         ),
-        in_specs=[SMEM] * 3 + [VMEM] * 5 + [pl.BlockSpec(memory_space=pl.ANY)],
+        in_specs=[SMEM] * 3 + [VMEM] * 5,
         out_specs=(VMEM,) * 3,
         scratch_shapes=[pltpu.VMEM((keys, 2 * HEAD_DIM), bf16), pltpu.VMEM((2 * HEAD_DIM, keys), bf16)],
         compiler_params=pltpu.CompilerParams(vmem_limit_bytes=40 * 1024 * 1024),
         cost_estimate=pl.CostEstimate(flops=12_000_000_000, bytes_accessed=4_000_000, transcendentals=5_000_000),
-    )(*numbers, queries, *kv_parts, held)
+    )(*numbers, queries, *kv_parts)
 
 
 def attend_grad(numbers, queries, kv_parts, grads, turned, lse):
@@ -655,9 +671,9 @@
     core = lax.axis_index("core").astype(jnp.int32).reshape(1)
     place = lax.axis_index("x").astype(jnp.int32).reshape(1)
     me = lax.axis_index(("yl", "core")).astype(jnp.int32).reshape(1)
-    (small_shard,) = call(
+    small_shard, by_head = call(
         shard_kernel,
-        [((shard_rows + 16, 4 * HEAD_DIM + 128), bf16)],
+        [((shard_rows + EXPERTS + 16, 4 * HEAD_DIM), bf16), ((shard_rows, KV_HEADS * 4 * HEAD_DIM), bf16)],
         (
             head.astype(jnp.int32).reshape(1), w_query, w_key, w_value, w_router,
             norm1_gain.reshape(1, -1), norm2_gain.reshape(1, -1),
@@ -666,9 +682,7 @@
         scalars=1,
     )
     small_pieces = pieces_direct(small_shard)
-    (copies,) = call(
-        copies_kernel, [((KV_HEADS, tokens, width), bf16)], (own_input,), 1_000_000, held=(small_shard,)
-    )
+    (copies,) = call(copies_kernel, [((KV_HEADS, tokens, width), bf16)], (own_input,), 1_000_000)
     group_input = exchange(copies.reshape(-1, width), ZY)
     head_w, router_w, gain_one, gain_two = call(
         small_kernel,
@@ -711,7 +725,7 @@
     )
     marked_arrived = exchange(marked_sent, CTX)
 
-    attn_group, attn_turned, lse = attend(numbers, queries, kv_parts, expert_other)
+    attn_group, attn_turned, lse = attend(numbers, queries, kv_parts)
 
     out_pieces = pieces_by_row(w_out, out_other)
 
@@ -736,25 +750,23 @@
     )
     arrived = exchange(outgoing, CTX)
 
-    hidden_units = w_gate.shape[2]
     expert_out, in_grad, pre_grad, inner_act, route_grad = run_experts(
         expert, me, arrived, marked_arrived, expert_pieces, router_w
     )
     back = exchange(in_grad, CTX)
-    grad_gu = product_tn(arrived, pre_grad).astype(bf16).reshape(4, -1, 2 * hidden_units)
-    grad_down = product_tn(inner_act, route_grad).astype(bf16).reshape(4, -1, width)
-    expert_both = scatter_core(jnp.concatenate([grad_gu, grad_down], axis=1))
-    by_head = jnp.concatenate(
-        [
-            w_query.reshape(shard_rows, KV_HEADS, 2 * HEAD_DIM),
-            w_key.reshape(shard_rows, KV_HEADS, HEAD_DIM),
-            w_value.reshape(shard_rows, KV_HEADS, HEAD_DIM),
-        ],
-        axis=2,
-    ).reshape(shard_rows, -1)
-    by_head = tie(by_head, arrived)
-    head_pieces = pieces_by_row(by_head, swap(by_head, "yl"))
-    expert_sums = scatter_row(expert_both)
+    by_head_sent = tie(by_head, normed2)
+    head_pieces = pieces_by_row(by_head_sent, swap(by_head_sent, "yl"))
+    expert_shape = ((2, *expert_shard.shape), bf16)
+    expert_both = join_core(
+        *call(
+            expert_grad_kernel,
+            [expert_shape, expert_shape],
+            (core, arrived, pre_grad, inner_act, route_grad),
+            5_000_000_000,
+            held=(head_pieces[2],),
+            scalars=1,
+        )
+    )
 
     hidden_grad, branch_grad, logit_grad, gain_two_grad, attn_grad = call(
         token_grad_kernel,
@@ -767,13 +779,13 @@
         ],
         (me, fetch, back, gate_probs, router_w, hidden, gain_two, cotangent[0], *out_pieces),
         800_000_000,
-        held=(expert_sums, *head_pieces),
+        held=(expert_both, *head_pieces),
         scalars=1,
     )
 
     group_grad = exchange(attn_grad.reshape(KV_HEADS * tokens, 2 * HEAD_DIM), ZY)
     dq, *dkv_parts = attend_grad(numbers, queries, kv_parts, group_grad, attn_turned, lse)
-    returned = exchange(tie(expert_out, group_grad), CTX)
+    expert_sums = scatter_row(tie(expert_both, group_grad))
     dkv_turned = [turn(dkv_parts[step], "x", -step) for step in (1, 2, 3)]
     dense_shape = ((2, shard_rows, width + 128), bf16)
     dense_both = join_core(
@@ -782,18 +794,19 @@
             [dense_shape, dense_shape],
             (core, attn_rows, branch_grad, normed2, logit_grad, gain_two_grad),
             400_000_000,
-            held=tuple(dkv_turned),
             scalars=1,
         )
     )
-    dense = scatter_row(dense_both)
+    dense = scatter_row(dense_both).astype(bf16)
+    dense = exchange(dense, CTX).reshape(EXPERTS, -1, width + 128)
+    dense = jnp.sum(dense.astype(f32), axis=0).astype(bf16)
 
     (grads,) = call(
         head_grad_kernel,
         [((KV_HEADS * tokens, 4 * HEAD_DIM), bf16)],
         (dq, dkv_parts[0], *dkv_turned, cosine, sine),
         100_000_000,
-        held=(returned,),
+        held=(dense, expert_sums),
     )
     token_grads = exchange(grads, ZY)
     head_shape = ((2, shard_rows, 4 * HEAD_DIM), bf16)
@@ -802,8 +815,7 @@
     )
     head_part = scatter_row(head_both).astype(bf16)
 
-    dense = exchange(tie(dense.astype(bf16), token_grads, head_part), CTX).reshape(EXPERTS, -1, width + 128)
-    dense = jnp.sum(dense.astype(f32), axis=0).astype(bf16)
+    returned = exchange(tie(expert_out, token_grads), CTX)
 
     gain_shape = ((1, shard_rows), f32)
     input_grad, *gain_parts = call(
@@ -823,8 +835,9 @@
     (last,) = call(
         pack_kernel,
         [((KV_HEADS, shard_rows // 4 + 32, width + 128), bf16)],
-        (place, *all_x(tie(head_part, gain_parts[0])), *all_x(tie(gain_sum, dense)), *all_x(dense)),
+        (place, *all_x(head_part), *all_x(gain_sum), *all_x(dense)),
         1_000_000,
+        held=(returned,),
         scalars=1,
         scratch=[(32, width + 128)],
     )
@@ -862,8 +875,8 @@
         grad_out,
         gain_two_grad.reshape(-1),
         grad_router,
-        expert_sums[None, :shard_rows, :hidden_units],
-        expert_sums[None, :shard_rows, hidden_units:],
+        expert_sums[None, :shard_rows, : width // 2],
+        expert_sums[None, :shard_rows, width // 2 :],
         expert_sums[None, shard_rows:],
     )
 

time: 539 us -> 519 us (0.963)
  waiting for transfers between devices: 198 us -> 182 us
  matrix products: 18.1 us -> 2.19 us
  Pallas kernels: 93.4 us -> 109 us
  starting transfers between devices: 95.9 us -> 111 us
  local copies, waits for them, and re-layouts: 71.7 us -> 65.6 us
    ppermute x15, waiting for transfers between devices: 83.5 us -> 35.2 us  [swap(): return lax.ppermute(values, axis, [(0, 1), (1, 0)])]
    all_to_all x9, waiting for transfers between devices: 77.4 us -> 121 us  [exchange(): lax.all_to_all(rows_first(values), axes, 0, 0, tiled=True)]
    pallas_call x12 -> x13, Pallas kernels: 23.7 us -> 39.1 us  [call(): pl.pallas_call(body, out_shape=tuple((jax.ShapeDtypeStruct(shape, dtype)...]
    dot_general x2 -> x0, matrix products: 12 us -> none  [product_tn(): lax.dot_general(left, right, (((0,), (0,)), ((), ())), preferred_element_...]
    ppermute x15, waiting for transfers between devices: 22.7 us -> 12.9 us  [turn(): return lax.ppermute(values, axis, [(i, (i + step) % 4) for i in range(4)])]
    ppermute x15, starting transfers between devices: 23.1 us -> 31.1 us  [turn(): return lax.ppermute(values, axis, [(i, (i + step) % 4) for i in range(4)])]
    ppermute x15, starting transfers between devices: 8.02 us -> 15.5 us  [swap(): return lax.ppermute(values, axis, [(0, 1), (1, 0)])]
  transfers between devices with their start and end apart: 45 -> 45, of which waited for: 19 -> 19; matrix products, arithmetic and copies ran while one was open for 11% -> 9% of each run, Pallas kernels for 11% -> 17%
where the time goes in v1:
time: 519 us; the launch traced here: 512 us
  waiting for transfers between devices  182 us (35%)
  starting transfers between devices  111 us (21%)
  Pallas kernels  109 us (21%)
  local copies, waits for them, and re-layouts  65.6 us (13%)
  other arithmetic  20.8 us (4%)
  blocking collectives  18.1 us (3%)
    all_to_all x9, waiting for transfers between devices, exchange(): lax.all_to_all(rows_first(values), axes, 0, 0, tiled=True)  121 us
    all_to_all x9, starting transfers between devices, exchange(): lax.all_to_all(rows_first(values), axes, 0, 0, tiled=True)  60.2 us
    pallas_call x13, Pallas kernels, call(): pl.pallas_call(body, out_shape=tuple((jax.ShapeDtypeStruct(shape, dtype)...  39.1 us
    unnamed x164, local copies, waits for them, and re-layouts  37.9 us
    ppermute x15, waiting for transfers between devices, swap(): return lax.ppermute(values, axis, [(0, 1), (1, 0)])  35.2 us
    ppermute x15, starting transfers between devices, turn(): return lax.ppermute(values, axis, [(i, (i + step) % 4) for i in range(4)])  31.1 us
    pallas_call x1, Pallas kernels, attend(): pl.pallas_call(attend_kernel, out_shape=(jax.ShapeDtypeStruct((rows, 2 *...  23.3 us
    pallas_call x1, Pallas kernels, attend_grad(): pl.pallas_call(attend_grad_kernel, out_shape=(jax.ShapeDtypeStruct((rows,...  22.8 us
  transfers between devices with their start and end apart: 45, of which 19 were waited for; matrix products, arithmetic and copies ran while one was open for 9% of the time, Pallas kernels for 17%

profile of v1, /device:TPU:0, one launch (start us, length us, event | category | flops | bytes accessed | tf_op | source)
XLA Modules:
  0.0 512.4 jit_solution(6970535041409905149)
XLA Ops:
  1.6 1.5 shard_map.229
  3.1 8.2 %all-to-all-start = ((bf16[8,128,1024]{2,1,0:T(8,128)(2,1)}), bf16[8,128,1024]{2,1,0:T(8,128)(2,1)}, u32[]{:S(2)}, u32[]{:S(2)}) async-start(bf16[8,128,1024]{2,1,0:T(8,128)(2,1)} %shard_map.229), calls=%async_computation | async-start | bytes 4194304 | tf_op jit(solution)/shard_map/all_to_all | solution.py:58
  18.4 3.0 multiply_sine_fusion
  21.5 3.3 concatenate.22.cos_ref.refs_5_
  25.6 3.9 concatenate.24.sin_ref.refs_6_
  29.5 10.2 %collective-permute-done.1.refs_3_ = bf16[304,256]{1,0:T(8,128)(2,1)} collective-permute-done((bf16[304,256]{1,0:T(8,128)(2,1)}, bf16[304,256]{1,0:T(8,128)(2,1)}, u32[]{:S(2)}, u32[]{:S(2)}) %collective-permute-start.1) | collective-permute-done | bytes 155680 | tf_op jit(solution)/shard_map/ppermute | solution.py:71
  39.8 2.4 collective-permute-done.2.refs_4_
  46.0 4.5 shard_map.232
  52.5 1.5 collective-permute-start.3
  54.0 2.7 collective-permute-start.4
  56.7 1.4 collective-permute-start.5
  60.0 9.9 %collective-permute-done.6.refs_5_.refs_4_.refs_10_ = bf16[256,1024]{1,0:T(8,128)(2,1)S(1)} collective-permute-done((bf16[256,1024]{1,0:T(8,128)(2,1)}, bf16[256,1024]{1,0:T(8,128)(2,1)S(1)}, u32[]{:S(2)}, u32[]{:S(2)}) %collective-permute-start.6) | collective-permute-done | bytes 524320 | tf_op jit(solution)/shard_map/ppermute | solution.py:46
  70.0 2.9 shard_map.234
  72.8 11.0 %all-to-all-start.1 = ((bf16[32,48,1152]{2,1,0:T(8,128)(2,1)}), bf16[32,48,1152]{2,1,0:T(8,128)(2,1)}, u32[]{:S(2)}, u32[]{:S(2)}) async-start(bf16[32,48,1152]{2,1,0:T(8,128)(2,1)} %bitcast.103), calls=%async_computation.1 | async-start | bytes 7077888 | tf_op jit(solution)/shard_map/all_to_all | solution.py:58
  86.5 23.3 %shard_map.233 = (bf16[1024,128]{1,0:T(8,128)(2,1)S(1)}, f32[8,64,256]{2,1,0:T(8,128)S(1)}, f32[8,1,256]{2,1,0:T(1,128)S(1)}) custom-call(s32[16]{0:T(128)S(1)} %select_reduce_fusion.order_ref, s32[16]{0:T(128)S(1)} %lt.39.qnum_ref, s32[64]{0:T(128)S(1)} %reshape.203.knum_ref, bf16[1024,128]{1,0:T(8,128)(2,1)S(1)} %copy-done.55, ...), custom_call_target="tpu_custom_call" | custom-call | flops 12000000000 | bytes 4000000 | tf_op jit(solution)/shard_map/pallas_call | solution.py:603
  111.3 18.8 %all-to-all-done.1 = bf16[32,48,1152]{2,1,0:T(8,128)(2,1)} async-done(((bf16[32,48,1152]{2,1,0:T(8,128)(2,1)}), bf16[32,48,1152]{2,1,0:T(8,128)(2,1)}, u32[]{:S(2)}, u32[]{:S(2)}) %all-to-all-start.1) | async-done | bytes 3538976 | tf_op jit(solution)/shard_map/all_to_all | solution.py:58
  133.1 6.7 %all-to-all-start.2 = ((bf16[8,128,128]{2,1,0:T(8,128)(2,1)}), bf16[8,128,128]{2,1,0:T(8,128)(2,1)}, u32[]{:S(2)}, u32[]{:S(2)}) async-start(bf16[8,128,128]{2,1,0:T(8,128)(2,1)} %bitcast.100), calls=%async_computation.2 | async-start | bytes 524288 | tf_op jit(solution)/shard_map/all_to_all | solution.py:58
  139.9 8.9 %all-to-all-done.2.refs_1_ = bf16[8,128,128]{2,1,0:T(8,128)(2,1)} async-done(((bf16[8,128,128]{2,1,0:T(8,128)(2,1)}), bf16[8,128,128]{2,1,0:T(8,128)(2,1)}, u32[]{:S(2)}, u32[]{:S(2)}) %all-to-all-start.2) | async-done | bytes 262176 | tf_op jit(solution)/shard_map/all_to_all | solution.py:58
  148.8 4.8 shard_map.235
  154.9 5.2 %all-to-all-start.3 = ((bf16[32,48,1024]{2,1,0:T(8,128)(2,1)}), bf16[32,48,1024]{2,1,0:T(8,128)(2,1)}, u32[]{:S(2)}, u32[]{:S(2)}) async-start(bf16[32,48,1024]{2,1,0:T(8,128)(2,1)} %bitcast.106), calls=%async_computation.3 | async-start | bytes 6291456 | tf_op jit(solution)/shard_map/all_to_all | solution.py:58
  161.9 40.3 %all-to-all-done.3 = bf16[32,48,1024]{2,1,0:T(8,128)(2,1)} async-done(((bf16[32,48,1024]{2,1,0:T(8,128)(2,1)}), bf16[32,48,1024]{2,1,0:T(8,128)(2,1)}, u32[]{:S(2)}, u32[]{:S(2)}) %all-to-all-start.3) | async-done | bytes 3145760 | tf_op jit(solution)/shard_map/all_to_all | solution.py:58
  202.2 19.2 %shard_map.236 = (bf16[1536,1024]{1,0:T(8,128)(2,1)}, bf16[1536,1152]{1,0:T(8,128)(2,1)}, bf16[1536,1024]{1,0:T(8,128)(2,1)}, bf16[1536,512]{1,0:T(8,128)(2,1)}, bf16[1536,1024]{1,0:T(8,128)(2,1)}) custom-call(s32[1]{0:T(128)} %bitcast.23.expert_ref, s32[1]{0:T(128)} %bitcast.refs_0_.me_ref, bf16[1536,1024]{1,0:T(8,128)(2,1)} %bitcast.25.rows_ref.refs_1_, ...), custom_call_target="tpu_custom_call" | custom-call | flops 10000000000 | bytes 22000000 | tf_op jit(solution)/shard_map/pallas_call | solution.py:583
  221.3 7.5 %all-to-all-start.4 = ((bf16[32,48,1152]{2,1,0:T(8,128)(2,1)}), bf16[32,48,1152]{2,1,0:T(8,128)(2,1)}, u32[]{:S(2)}, u32[]{:S(2)}) async-start(bf16[32,48,1152]{2,1,0:T(8,128)(2,1)} %bitcast.104), calls=%async_computation.4 | async-start | bytes 7077888 | tf_op jit(solution)/shard_map/all_to_all | solution.py:58
  230.2 10.2 %shard_map.237 = (bf16[2,384,1024]{2,1,0:T(8,128)(2,1)S(1)}, bf16[2,384,1024]{2,1,0:T(8,128)(2,1)}) custom-call(s32[1]{0:T(128)} %bitcast.28.refs_0_, bf16[1536,1024]{1,0:T(8,128)(2,1)} %bitcast.25.rows_ref.refs_1_, bf16[1536,1024]{1,0:T(8,128)(2,1)} %get-tuple-element.75.refs_2_, bf16[1536,512]{1,0:T(8,128)(2,1)S(1)} %copy-done.63, ...), custom_call_target="tpu_custom_call" | custom-call | flops 5000000000 | bytes 8000000 | tf_op jit(solution)/shard_map/pallas_call | solution.py:349
  243.0 2.3 copy.60
  246.8 3.8 add_convert_fusion.refs_12_
  250.6 24.5 %all-to-all-done.4 = bf16[32,48,1152]{2,1,0:T(8,128)(2,1)} async-done(((bf16[32,48,1152]{2,1,0:T(8,128)(2,1)}), bf16[32,48,1152]{2,1,0:T(8,128)(2,1)}, u32[]{:S(2)}, u32[]{:S(2)}) %all-to-all-start.4) | async-done | bytes 3538976 | tf_op jit(solution)/shard_map/all_to_all | solution.py:58
  277.8 5.2 %shard_map.238 = (f32[128,1024]{1,0:T(8,128)S(1)}, bf16[128,1024]{1,0:T(8,128)(2,1)S(1)}, bf16[128,32]{1,0:T(8,128)(2,1)S(1)}, f32[1,1024]{1,0:T(1,128)S(1)}, bf16[8,128,128]{2,1,0:T(8,128)(2,1)}) custom-call(s32[1]{0:T(128)} %bitcast.refs_0_.me_ref, bf16[128,1536]{1,0:T(8,128)(2,1)S(1)} %compare_convert_fusion.refs_1_, bf16[1536,1152]{1,0:T(8,128)(2,1)} %bitcast.27.refs_2_, ...), custom_call_target="tpu_custom_call" | custom-call | flops 800000000 | bytes 8000000 | tf_op jit(solution)/shard_map/pallas_call | solution.py:349
  283.8 1.8 shard_map.240
  285.7 8.5 %collective-permute-start.19 = (bf16[2,256,1152]{2,1,0:T(8,128)(2,1)}, bf16[2,256,1152]{2,1,0:T(8,128)(2,1)}, u32[]{:S(2)}, u32[]{:S(2)}) collective-permute-start(bf16[2,256,1152]{2,1,0:T(8,128)(2,1)} %get-tuple-element.95), channel_id=1, source_target_pairs={{0,1},{1,0},{2,3},{3,2},{4,5},{5,4},{6,7},{7,6},{8,9},{9,8},{10,11... | collective-permute-start | bytes 3538952 | tf_op jit(solution)/shard_map/ppermute | solution.py:46
  294.2 3.2 collective-permute-done.19
  297.4 1.5 add_convert_fusion.1
  302.3 7.0 %all-to-all-start.5 = ((bf16[8,128,128]{2,1,0:T(8,128)(2,1)}), bf16[8,128,128]{2,1,0:T(8,128)(2,1)S(1)}, u32[]{:S(2)}, u32[]{:S(2)}) async-start(bf16[8,128,128]{2,1,0:T(8,128)(2,1)} %get-tuple-element.82), calls=%async_computation.5 | async-start | bytes 524288 | tf_op jit(solution)/shard_map/all_to_all | solution.py:58
  309.2 15.3 %all-to-all-done.5 = bf16[8,128,128]{2,1,0:T(8,128)(2,1)S(1)} async-done(((bf16[8,128,128]{2,1,0:T(8,128)(2,1)}), bf16[8,128,128]{2,1,0:T(8,128)(2,1)S(1)}, u32[]{:S(2)}, u32[]{:S(2)}) %all-to-all-start.5) | async-done | bytes 262176 | tf_op jit(solution)/shard_map/all_to_all | solution.py:58
  326.9 2.2 dynamic-slice_bitcast_fusion
  330.3 2.0 fusion.7
  332.3 6.3 %all-to-all-start.6 = ((bf16[32,8,1152]{2,1,0:T(8,128)(2,1)}), bf16[32,8,1152]{2,1,0:T(8,128)(2,1)}, u32[]{:S(2)}, u32[]{:S(2)}) async-start(bf16[32,8,1152]{2,1,0:T(8,128)(2,1)} %fusion.7), calls=%async_computation.6 | async-start | bytes 1179648 | tf_op jit(solution)/shard_map/all_to_all | solution.py:58
  338.7 22.8 %shard_map.239 = (f32[1024,128]{1,0:T(8,128)S(1)}, bf16[1024,128]{1,0:T(8,128)(2,1)S(1)}, bf16[1024,128]{1,0:T(8,128)(2,1)}, bf16[1024,128]{1,0:T(8,128)(2,1)}, bf16[1024,128]{1,0:T(8,128)(2,1)}) custom-call(s32[16]{0:T(128)S(1)} %copy-done.62, s32[16]{0:T(128)S(1)} %lt.39.qnum_ref, s32[64]{0:T(128)S(1)} %reshape.203.knum_ref, ...), custom_call_target="tpu_custom_call" | custom-call | flops 30000001024 | bytes 6000000 | tf_op jit(solution)/shard_map/pallas_call | solution.py:621
  362.2 3.5 collective-permute-start.16
  368.3 2.2 reduce_sum.42.refs_7_.refs_9_
  370.5 5.3 %collective-permute-done.16.refs_2_ = bf16[1024,128]{1,0:T(8,128)(2,1)} collective-permute-done((bf16[1024,128]{1,0:T(8,128)(2,1)}, bf16[1024,128]{1,0:T(8,128)(2,1)}, u32[]{:S(2)}, u32[]{:S(2)}) %collective-permute-start.16) | collective-permute-done | bytes 262176 | tf_op jit(solution)/shard_map/ppermute | solution.py:50
  376.7 2.8 collective-permute-done.18.refs_4_
  382.4 1.7 shard_map.241.refs_2_
  384.2 18.1 %all_to_all.120.refs_1_ = bf16[8,128,256]{2,1,0:T(8,128)(2,1)S(1)} all-to-all(bf16[8,128,256]{2,1,0:T(8,128)(2,1)S(1)} %bitcast.93), channel_id=1, replica_groups=mesh['x'=4,'z'=4,'yh'=2,'yl'=2,'core'=2] {'z','yh'}, dimensions={0} | all-to-all | bytes 1048576 | tf_op jit(solution)/shard_map/all_to_all | solution.py:58
  406.3 4.1 all-to-all-start.8
  411.5 1.6 copy-done.17
  414.0 1.5 collective-permute-done.22
  415.7 1.8 collective-permute-start.33
  417.5 2.8 collective-permute-start.34
  420.3 4.4 shard_map.242
  424.7 1.9 collective-permute-start.28
  426.6 20.4 %collective-permute-done.23 = bf16[256,256]{1,0:T(8,128)(2,1)S(1)} collective-permute-done((bf16[256,256]{1,0:T(8,128)(2,1)S(1)}, bf16[256,256]{1,0:T(8,128)(2,1)S(1)}, u32[]{:S(2)}, u32[]{:S(2)}) %collective-permute-start.23) | collective-permute-done | bytes 131104 | tf_op jit(solution)/shard_map/ppermute | solution.py:46
  448.0 8.7 %collective-permute-start.35 = (bf16[8,1152]{1,0:T(8,128)(2,1)S(1)}, bf16[8,1152]{1,0:T(8,128)(2,1)S(1)}, u32[]{:S(2)}, u32[]{:S(2)}) collective-permute-start(bf16[8,1152]{1,0:T(8,128)(2,1)S(1)} %copy-done.40), channel_id=1, source_target_pairs={{0,96},{32,0},{64,32},{96,64},{1,97},{33,1},{65,33},{97,65},{2,98}... | collective-permute-start | bytes 55304 | tf_op jit(solution)/shard_map/ppermute | solution.py:50
  456.7 1.5 collective-permute-start.25
  458.2 1.8 collective-permute-start.26
  462.9 2.1 collective-permute-start.31
  464.9 1.5 collective-permute-done.30.refs_6_
  467.9 2.0 collective-permute-done.32.refs_8_
  479.9 4.3 all-to-all-start.9
  486.1 2.3 copy.61
  488.4 2.0 slice_bitcast_fusion
  490.4 2.2 slice_bitcast_fusion.1
  495.0 13.1 %all-to-all-done.9.refs_0_ = bf16[8,96,1152]{2,1,0:T(8,128)(2,1)} async-done(((bf16[8,96,1152]{2,1,0:T(8,128)(2,1)}), bf16[8,96,1152]{2,1,0:T(8,128)(2,1)}, u32[]{:S(2)}, u32[]{:S(2)}) %all-to-all-start.9) | async-done | bytes 1769504 | tf_op jit(solution)/shard_map/all_to_all | solution.py:58
  508.1 3.4 shard_map.245
  (272 shorter events, 73.8 us)
Async XLA Ops:
  3.1 8.4 %copy-start.35 = (bf16[256,512]{1,0:T(8,128)(2,1)S(1)}, bf16[256,512]{1,0:T(8,128)(2,1)}, u32[]{:S(2)}) copy-start(bf16[256,512]{1,0:T(8,128)(2,1)} %refs_2_.2) | copy-start | bytes 786436
  3.1 8.4 %copy-start.36 = (bf16[256,512]{1,0:T(8,128)(2,1)S(1)}, bf16[256,512]{1,0:T(8,128)(2,1)}, u32[]{:S(2)}) copy-start(bf16[256,512]{1,0:T(8,128)(2,1)} %refs_3_.1) | copy-start | bytes 786436
  3.1 11.3 %copy-start.72 = (bf16[1,128,1024]{2,1,0:T(8,128)(2,1)S(1)}, bf16[1,128,1024]{2,1,0:T(8,128)(2,1)}, u32[]{:S(2)}) copy-start(bf16[1,128,1024]{2,1,0:T(8,128)(2,1)} %param.26) | copy-start | bytes 786436
  3.1 11.3 %copy-start.73 = (bf16[1,256,512]{2,1,0:T(8,128)(2,1)S(1)}, bf16[1,256,512]{2,1,0:T(8,128)(2,1)}, u32[]{:S(2)}) copy-start(bf16[1,256,512]{2,1,0:T(8,128)(2,1)} %param.25) | copy-start | bytes 786436
  3.1 11.3 %copy-start.74 = (bf16[1,256,512]{2,1,0:T(8,128)(2,1)S(1)}, bf16[1,256,512]{2,1,0:T(8,128)(2,1)}, u32[]{:S(2)}) copy-start(bf16[1,256,512]{2,1,0:T(8,128)(2,1)} %param.24) | copy-start | bytes 786436
  3.1 41.8 %all-to-all-start = ((bf16[8,128,1024]{2,1,0:T(8,128)(2,1)}), bf16[8,128,1024]{2,1,0:T(8,128)(2,1)}, u32[]{:S(2)}, u32[]{:S(2)}) async-start(bf16[8,128,1024]{2,1,0:T(8,128)(2,1)} %shard_map.229), calls=%async_computation | async-start | bytes 4194304 | tf_op jit(solution)/shard_map/all_to_all | solution.py:58
  12.5 17.0 %collective-permute-start = (bf16[304,256]{1,0:T(8,128)(2,1)}, bf16[304,256]{1,0:T(8,128)(2,1)}, u32[]{:S(2)}, u32[]{:S(2)}) collective-permute-start(bf16[304,256]{1,0:T(8,128)(2,1)} %get-tuple-element.62.refs_1_), channel_id=1, source_target_pairs={{0,1},{1,0},{2,3},{3,2},{4,5},{5,4},{6,7},{7,6},{8,9},{9,8},{10,11... | collective-permute-start | bytes 466952 | tf_op jit(solution)/shard_map/ppermute | solution.py:71
  12.5 27.2 %collective-permute-start.1 = (bf16[304,256]{1,0:T(8,128)(2,1)}, bf16[304,256]{1,0:T(8,128)(2,1)}, u32[]{:S(2)}, u32[]{:S(2)}) collective-permute-start(bf16[304,256]{1,0:T(8,128)(2,1)} %get-tuple-element.62.refs_1_), channel_id=1, source_target_pairs={{0,2},{1,3},{2,0},{3,1},{4,6},{5,7},{6,4},{7,5},{8,10},{9,11},{10,... | collective-permute-start | bytes 466952 | tf_op jit(solution)/shard_map/ppermute | solution.py:71
  13.2 28.9 %collective-permute-start.2 = (bf16[304,256]{1,0:T(8,128)(2,1)}, bf16[304,256]{1,0:T(8,128)(2,1)}, u32[]{:S(2)}, u32[]{:S(2)}) collective-permute-start(bf16[304,256]{1,0:T(8,128)(2,1)} %get-tuple-element.62.refs_1_), channel_id=1, source_target_pairs={{0,3},{1,2},{2,1},{3,0},{4,7},{5,6},{6,5},{7,4},{8,11},{9,10},{10,... | collective-permute-start | bytes 466952 | tf_op jit(solution)/shard_map/ppermute | solution.py:71
  15.4 54.6 %collective-permute-start.7 = (bf16[384,1024]{1,0:T(8,128)(2,1)}, bf16[384,1024]{1,0:T(8,128)(2,1)S(1)}, u32[]{:S(2)}, u32[]{:S(2)}) collective-permute-start(bf16[384,1024]{1,0:T(8,128)(2,1)} %pad_maximum_fusion.refs_11_.piece0), channel_id=1, source_target_pairs={{0,2},{2,0},{1,3},{3,1},{4,6},{6,4},{5,7},{7,5},{8,10},{10,8},{9,1... | collective-permute-start | bytes 2359304 | tf_op jit(solution)/shard_map/ppermute | solution.py:46
  16.0 53.9 %collective-permute-start.6 = (bf16[256,1024]{1,0:T(8,128)(2,1)}, bf16[256,1024]{1,0:T(8,128)(2,1)S(1)}, u32[]{:S(2)}, u32[]{:S(2)}) collective-permute-start(bf16[256,1024]{1,0:T(8,128)(2,1)} %refs_8_.1), channel_id=1, source_target_pairs={{0,2},{2,0},{1,3},{3,1},{4,6},{6,4},{5,7},{7,5},{8,10},{10,8},{9,1... | collective-permute-start | bytes 1572872 | tf_op jit(solution)/shard_map/ppermute | solution.py:46
  29.5 21.0 %copy-start.1 = (f32[1024,256]{1,0:T(8,128)}, f32[1024,256]{1,0:T(8,128)S(1)}, u32[]{:S(2)}) copy-start(f32[1024,256]{1,0:T(8,128)S(1)} %concatenate.24.sin_ref.refs_6_) | copy-start | bytes 3145732
  52.5 17.4 %collective-permute-start.3 = (bf16[1024,128]{1,0:T(8,128)(2,1)}, bf16[1024,128]{1,0:T(8,128)(2,1)}, u32[]{:S(2)}, u32[]{:S(2)}) collective-permute-start(bf16[1024,128]{1,0:T(8,128)(2,1)} %get-tuple-element.66.kv0), channel_id=1, source_target_pairs={{0,32},{32,64},{64,96},{96,0},{1,33},{33,65},{65,97},{97,1},{2,34}... | collective-permute-start | bytes 786440 | tf_op jit(solution)/shard_map/ppermute | solution.py:50
  54.0 16.0 %collective-permute-start.4 = (bf16[1024,128]{1,0:T(8,128)(2,1)}, bf16[1024,128]{1,0:T(8,128)(2,1)}, u32[]{:S(2)}, u32[]{:S(2)}) collective-permute-start(bf16[1024,128]{1,0:T(8,128)(2,1)} %get-tuple-element.66.kv0), channel_id=1, source_target_pairs={{0,64},{32,96},{64,0},{96,32},{1,65},{33,97},{65,1},{97,33},{2,66}... | collective-permute-start | bytes 786440 | tf_op jit(solution)/shard_map/ppermute | solution.py:50
  56.7 13.2 %collective-permute-start.5 = (bf16[1024,128]{1,0:T(8,128)(2,1)}, bf16[1024,128]{1,0:T(8,128)(2,1)}, u32[]{:S(2)}, u32[]{:S(2)}) collective-permute-start(bf16[1024,128]{1,0:T(8,128)(2,1)} %get-tuple-element.66.kv0), channel_id=1, source_target_pairs={{0,96},{32,0},{64,32},{96,64},{1,97},{33,1},{65,33},{97,65},{2,98}... | collective-permute-start | bytes 786440 | tf_op jit(solution)/shard_map/ppermute | solution.py:50
  69.9 15.2 %copy-start.10 = (bf16[384,1024]{1,0:T(8,128)(2,1)}, bf16[384,1024]{1,0:T(8,128)(2,1)S(1)}, u32[]{:S(2)}) copy-start(bf16[384,1024]{1,0:T(8,128)(2,1)S(1)} %collective-permute-done.7.refs_6_.refs_13_.piece2) | copy-start | bytes 2359300
  72.8 57.2 %all-to-all-start.1 = ((bf16[32,48,1152]{2,1,0:T(8,128)(2,1)}), bf16[32,48,1152]{2,1,0:T(8,128)(2,1)}, u32[]{:S(2)}, u32[]{:S(2)}) async-start(bf16[32,48,1152]{2,1,0:T(8,128)(2,1)} %bitcast.103), calls=%async_computation.1 | async-start | bytes 7077888 | tf_op jit(solution)/shard_map/all_to_all | solution.py:58
  83.8 56.1 %collective-permute-start.10 = (bf16[384,1024]{1,0:T(8,128)(2,1)}, bf16[384,1024]{1,0:T(8,128)(2,1)}, u32[]{:S(2)}, u32[]{:S(2)}) collective-permute-start(bf16[384,1024]{1,0:T(8,128)(2,1)} %pad_maximum_fusion.refs_11_.piece0), channel_id=1, source_target_pairs={{0,1},{1,0},{2,3},{3,2},{4,5},{5,4},{6,7},{7,6},{8,9},{9,8},{10,11... | collective-permute-start | bytes 2359304 | tf_op jit(solution)/shard_map/ppermute | solution.py:46
  83.9 56.0 %collective-permute-start.8 = (bf16[256,1024]{1,0:T(8,128)(2,1)}, bf16[256,1024]{1,0:T(8,128)(2,1)}, u32[]{:S(2)}, u32[]{:S(2)}) collective-permute-start(bf16[256,1024]{1,0:T(8,128)(2,1)} %refs_8_.1), channel_id=1, source_target_pairs={{0,1},{1,0},{2,3},{3,2},{4,5},{5,4},{6,7},{7,6},{8,9},{9,8},{10,11... | collective-permute-start | bytes 1572872 | tf_op jit(solution)/shard_map/ppermute | solution.py:46
  84.9 24.9 %copy-start.61 = (s32[16]{0:T(128)}, s32[16]{0:T(128)S(1)}, u32[]{:S(2)}) copy-start(s32[16]{0:T(128)S(1)} %select_reduce_fusion.order_ref) | copy-start | bytes 196
  84.9 55.0 %collective-permute-start.9 = (bf16[256,1024]{1,0:T(8,128)(2,1)S(1)}, bf16[256,1024]{1,0:T(8,128)(2,1)}, u32[]{:S(2)}, u32[]{:S(2)}) collective-permute-start(bf16[256,1024]{1,0:T(8,128)(2,1)S(1)} %collective-permute-done.6.refs_5_.refs_4_.refs_10_), channel_id=1, source_target_pairs={{0,1},{1,0},{2,3},{3,2},{4,5},{5,4},{6,7},{7,6},{8,9},{9,8},{10,11... | collective-permute-start | bytes 1572872 | tf_op jit(solution)/shard_map/ppermute | solution.py:46
  85.1 54.8 %collective-permute-start.11 = (bf16[384,1024]{1,0:T(8,128)(2,1)S(1)}, bf16[384,1024]{1,0:T(8,128)(2,1)}, u32[]{:S(2)}, u32[]{:S(2)}) collective-permute-start(bf16[384,1024]{1,0:T(8,128)(2,1)S(1)} %collective-permute-done.7.refs_6_.refs_13_.piece2), channel_id=1, source_target_pairs={{0,1},{1,0},{2,3},{3,2},{4,5},{5,4},{6,7},{7,6},{8,9},{9,8},{10,11... | collective-permute-start | bytes 2359304 | tf_op jit(solution)/shard_map/ppermute | solution.py:46
  86.5 62.3 %copy-start.12 = (bf16[1,128,1024]{2,1,0:T(8,128)(2,1)S(1)}, bf16[1,128,1024]{2,1,0:T(8,128)(2,1)}, u32[]{:S(2)}) copy-start(bf16[1,128,1024]{2,1,0:T(8,128)(2,1)} %param.14) | copy-start | bytes 786436
  86.5 62.3 %copy-start.22 = (bf16[1024,32]{1,0:T(8,128)(2,1)S(1)}, bf16[1024,32]{1,0:T(8,128)(2,1)}, u32[]{:S(2)}) copy-start(bf16[1024,32]{1,0:T(8,128)(2,1)} %copy-done.21) | copy-start | bytes 196612
  111.3 37.5 %copy-start.66 = (f32[8,1,256]{2,1,0:T(1,128)}, f32[8,1,256]{2,1,0:T(1,128)S(1)}, u32[]{:S(2)}) copy-start(f32[8,1,256]{2,1,0:T(1,128)S(1)} %get-tuple-element.84.lse_ref) | copy-start | bytes 24580
  133.1 15.6 %all-to-all-start.2 = ((bf16[8,128,128]{2,1,0:T(8,128)(2,1)}), bf16[8,128,128]{2,1,0:T(8,128)(2,1)}, u32[]{:S(2)}, u32[]{:S(2)}) async-start(bf16[8,128,128]{2,1,0:T(8,128)(2,1)} %bitcast.100), calls=%async_computation.2 | async-start | bytes 524288 | tf_op jit(solution)/shard_map/all_to_all | solution.py:58
  154.9 120.2 %copy-start.18 = (f32[128,1024]{1,0:T(8,128)}, f32[128,1024]{1,0:T(8,128)S(1)}, u32[]{:S(2)}) copy-start(f32[128,1024]{1,0:T(8,128)S(1)} %get-tuple-element.70.refs_5_) | copy-start | bytes 1572868
  154.9 47.2 %all-to-all-start.3 = ((bf16[32,48,1024]{2,1,0:T(8,128)(2,1)}), bf16[32,48,1024]{2,1,0:T(8,128)(2,1)}, u32[]{:S(2)}, u32[]{:S(2)}) async-start(bf16[32,48,1024]{2,1,0:T(8,128)(2,1)} %bitcast.106), calls=%async_computation.3 | async-start | bytes 6291456 | tf_op jit(solution)/shard_map/all_to_all | solution.py:58
  161.3 113.7 %copy-start.8 = (bf16[256,2048]{1,0:T(8,128)(2,1)}, bf16[256,2048]{1,0:T(8,128)(2,1)S(1)}, u32[]{:S(2)}) copy-start(bf16[256,2048]{1,0:T(8,128)(2,1)S(1)} %constant_dynamic-update-slice_fusion.1.refs_13_.refs_2_) | copy-start | bytes 3145732
  161.4 67.5 %collective-permute-start.12 = (bf16[256,2048]{1,0:T(8,128)(2,1)S(1)}, bf16[256,2048]{1,0:T(8,128)(2,1)}, u32[]{:S(2)}, u32[]{:S(2)}) collective-permute-start(bf16[256,2048]{1,0:T(8,128)(2,1)S(1)} %constant_dynamic-update-slice_fusion.1.refs_13_.refs_2_), channel_id=1, source_target_pairs={{0,2},{2,0},{1,3},{3,1},{4,6},{6,4},{5,7},{7,5},{8,10},{10,8},{9,1... | collective-permute-start | bytes 3145736 | tf_op jit(solution)/shard_map/ppermute | solution.py:46
  221.3 53.7 %all-to-all-start.4 = ((bf16[32,48,1152]{2,1,0:T(8,128)(2,1)}), bf16[32,48,1152]{2,1,0:T(8,128)(2,1)}, u32[]{:S(2)}, u32[]{:S(2)}) async-start(bf16[32,48,1152]{2,1,0:T(8,128)(2,1)} %bitcast.104), calls=%async_computation.4 | async-start | bytes 7077888 | tf_op jit(solution)/shard_map/all_to_all | solution.py:58
  241.5 5.3 %collective-permute-start.13 = (bf16[2,384,1024]{2,1,0:T(8,128)(2,1)}, bf16[2,384,1024]{2,1,0:T(8,128)(2,1)}, u32[]{:S(2)}, u32[]{:S(2)}) collective-permute-start(bf16[2,384,1024]{2,1,0:T(8,128)(2,1)} %get-tuple-element.81), channel_id=1, source_target_pairs={{0,1},{1,0},{2,3},{3,2},{4,5},{5,4},{6,7},{7,6},{8,9},{9,8},{10,11... | collective-permute-start | bytes 4718600 | tf_op jit(solution)/shard_map/ppermute | solution.py:46
  241.5 9.1 %collective-permute-start.14 = (bf16[256,2048]{1,0:T(8,128)(2,1)S(1)}, bf16[256,2048]{1,0:T(8,128)(2,1)}, u32[]{:S(2)}, u32[]{:S(2)}) collective-permute-start(bf16[256,2048]{1,0:T(8,128)(2,1)S(1)} %constant_dynamic-update-slice_fusion.1.refs_13_.refs_2_), channel_id=1, source_target_pairs={{0,1},{1,0},{2,3},{3,2},{4,5},{5,4},{6,7},{7,6},{8,9},{9,8},{10,11... | collective-permute-start | bytes 3145736 | tf_op jit(solution)/shard_map/ppermute | solution.py:46
  242.1 8.5 %collective-permute-start.15 = (bf16[256,2048]{1,0:T(8,128)(2,1)}, bf16[256,2048]{1,0:T(8,128)(2,1)}, u32[]{:S(2)}, u32[]{:S(2)}) collective-permute-start(bf16[256,2048]{1,0:T(8,128)(2,1)} %collective-permute-done.12.refs_5_.refs_15_.refs_4_), channel_id=1, source_target_pairs={{0,1},{1,0},{2,3},{3,2},{4,5},{5,4},{6,7},{7,6},{8,9},{9,8},{10,11... | collective-permute-start | bytes 3145736 | tf_op jit(solution)/shard_map/ppermute | solution.py:46
  285.7 11.7 %collective-permute-start.19 = (bf16[2,256,1152]{2,1,0:T(8,128)(2,1)}, bf16[2,256,1152]{2,1,0:T(8,128)(2,1)}, u32[]{:S(2)}, u32[]{:S(2)}) collective-permute-start(bf16[2,256,1152]{2,1,0:T(8,128)(2,1)} %get-tuple-element.95), channel_id=1, source_target_pairs={{0,1},{1,0},{2,3},{3,2},{4,5},{5,4},{6,7},{7,6},{8,9},{9,8},{10,11... | collective-permute-start | bytes 3538952 | tf_op jit(solution)/shard_map/ppermute | solution.py:46
  300.8 29.5 %collective-permute-start.20 = (bf16[256,1152]{1,0:T(8,128)(2,1)}, bf16[256,1152]{1,0:T(8,128)(2,1)}, u32[]{:S(2)}, u32[]{:S(2)}) collective-permute-start(bf16[256,1152]{1,0:T(8,128)(2,1)} %dynamic-slice_bitcast_fusion.1), channel_id=1, source_target_pairs={{0,2},{2,0},{1,3},{3,1},{4,6},{6,4},{5,7},{7,5},{8,10},{10,8},{9,1... | collective-permute-start | bytes 1769480 | tf_op jit(solution)/shard_map/ppermute | solution.py:46
  302.3 22.3 %all-to-all-start.5 = ((bf16[8,128,128]{2,1,0:T(8,128)(2,1)}), bf16[8,128,128]{2,1,0:T(8,128)(2,1)S(1)}, u32[]{:S(2)}, u32[]{:S(2)}) async-start(bf16[8,128,128]{2,1,0:T(8,128)(2,1)} %get-tuple-element.82), calls=%async_computation.5 | async-start | bytes 524288 | tf_op jit(solution)/shard_map/all_to_all | solution.py:58
  329.1 9.6 %copy-start.56 = (bf16[1024,128]{1,0:T(8,128)(2,1)S(1)}, bf16[1024,128]{1,0:T(8,128)(2,1)}, u32[]{:S(2)}) copy-start(bf16[1024,128]{1,0:T(8,128)(2,1)} %copy-done.54) | copy-start | bytes 786436
  329.1 9.6 %copy-start.62 = (s32[16]{0:T(128)S(1)}, s32[16]{0:T(128)}, u32[]{:S(2)}) copy-start(s32[16]{0:T(128)} %copy-done.61) | copy-start | bytes 196
  329.1 9.6 %copy-start.65 = (f32[8,64,256]{2,1,0:T(8,128)S(1)}, f32[8,64,256]{2,1,0:T(8,128)}, u32[]{:S(2)}) copy-start(f32[8,64,256]{2,1,0:T(8,128)} %copy-done.64) | copy-start | bytes 1572868
  329.1 9.6 %copy-start.67 = (f32[8,1,256]{2,1,0:T(1,128)S(1)}, f32[8,1,256]{2,1,0:T(1,128)}, u32[]{:S(2)}) copy-start(f32[8,1,256]{2,1,0:T(1,128)} %copy-done.66) | copy-start | bytes 24580
  329.1 37.8 %collective-permute-start.21 = (bf16[384,1024]{1,0:T(8,128)(2,1)}, bf16[384,1024]{1,0:T(8,128)(2,1)}, u32[]{:S(2)}, u32[]{:S(2)}) collective-permute-start(bf16[384,1024]{1,0:T(8,128)(2,1)} %dynamic-slice_bitcast_fusion), channel_id=1, source_target_pairs={{0,2},{2,0},{1,3},{3,1},{4,6},{6,4},{5,7},{7,5},{8,10},{10,8},{9,1... | collective-permute-start | bytes 2359304 | tf_op jit(solution)/shard_map/ppermute | solution.py:46
  332.3 36.0 %all-to-all-start.6 = ((bf16[32,8,1152]{2,1,0:T(8,128)(2,1)}), bf16[32,8,1152]{2,1,0:T(8,128)(2,1)}, u32[]{:S(2)}, u32[]{:S(2)}) async-start(bf16[32,8,1152]{2,1,0:T(8,128)(2,1)} %fusion.7), calls=%async_computation.6 | async-start | bytes 1179648 | tf_op jit(solution)/shard_map/all_to_all | solution.py:58
  338.7 28.2 %copy-start.68 = (bf16[2,384,1024]{2,1,0:T(8,128)(2,1)S(1)}, bf16[2,384,1024]{2,1,0:T(8,128)(2,1)}, u32[]{:S(2)}) copy-start(bf16[2,384,1024]{2,1,0:T(8,128)(2,1)} %fusion.18) | copy-start | bytes 4718596
  362.2 13.6 %collective-permute-start.16 = (bf16[1024,128]{1,0:T(8,128)(2,1)}, bf16[1024,128]{1,0:T(8,128)(2,1)}, u32[]{:S(2)}, u32[]{:S(2)}) collective-permute-start(bf16[1024,128]{1,0:T(8,128)(2,1)} %get-tuple-element.87), channel_id=1, source_target_pairs={{0,96},{32,0},{64,32},{96,64},{1,97},{33,1},{65,33},{97,65},{2,98}... | collective-permute-start | bytes 786440 | tf_op jit(solution)/shard_map/ppermute | solution.py:50
  365.7 11.1 %collective-permute-start.17 = (bf16[1024,128]{1,0:T(8,128)(2,1)}, bf16[1024,128]{1,0:T(8,128)(2,1)}, u32[]{:S(2)}, u32[]{:S(2)}) collective-permute-start(bf16[1024,128]{1,0:T(8,128)(2,1)} %get-tuple-element.88), channel_id=1, source_target_pairs={{0,64},{32,96},{64,0},{96,32},{1,65},{33,97},{65,1},{97,33},{2,66}... | collective-permute-start | bytes 786440 | tf_op jit(solution)/shard_map/ppermute | solution.py:50
  366.5 13.0 %collective-permute-start.18 = (bf16[1024,128]{1,0:T(8,128)(2,1)}, bf16[1024,128]{1,0:T(8,128)(2,1)}, u32[]{:S(2)}, u32[]{:S(2)}) collective-permute-start(bf16[1024,128]{1,0:T(8,128)(2,1)} %get-tuple-element.89), channel_id=1, source_target_pairs={{0,32},{32,64},{64,96},{96,0},{1,33},{33,65},{65,97},{97,1},{2,34}... | collective-permute-start | bytes 786440 | tf_op jit(solution)/shard_map/ppermute | solution.py:50
  368.3 15.9 %copy-start = (f32[384,1024]{1,0:T(8,128)}, f32[384,1024]{1,0:T(8,128)S(1)}, u32[]{:S(2)}) copy-start(f32[384,1024]{1,0:T(8,128)S(1)} %convert_add_fusion.refs_8_) | copy-start | bytes 4718596
  406.3 65.6 %all-to-all-start.8 = ((bf16[32,48,1024]{2,1,0:T(8,128)(2,1)}), bf16[32,48,1024]{2,1,0:T(8,128)(2,1)S(1)}, u32[]{:S(2)}, u32[]{:S(2)}) async-start(bf16[32,48,1024]{2,1,0:T(8,128)(2,1)} %bitcast.105), calls=%async_computation.8 | async-start | bytes 6291456 | tf_op jit(solution)/shard_map/all_to_all | solution.py:58
  413.9 1.6 collective-permute-start.22
  415.6 31.4 %collective-permute-start.23 = (bf16[256,256]{1,0:T(8,128)(2,1)S(1)}, bf16[256,256]{1,0:T(8,128)(2,1)S(1)}, u32[]{:S(2)}, u32[]{:S(2)}) collective-permute-start(bf16[256,256]{1,0:T(8,128)(2,1)S(1)} %dynamic-slice_bitcast_fusion.2), channel_id=1, source_target_pairs={{0,2},{2,0},{1,3},{3,1},{4,6},{6,4},{5,7},{7,5},{8,10},{10,8},{9,1... | collective-permute-start | bytes 393224 | tf_op jit(solution)/shard_map/ppermute | solution.py:46
  415.7 31.7 %collective-permute-start.33 = (bf16[8,1152]{1,0:T(8,128)(2,1)S(1)}, bf16[8,1152]{1,0:T(8,128)(2,1)S(1)}, u32[]{:S(2)}, u32[]{:S(2)}) collective-permute-start(bf16[8,1152]{1,0:T(8,128)(2,1)S(1)} %copy-done.40), channel_id=1, source_target_pairs={{0,32},{32,64},{64,96},{96,0},{1,33},{33,65},{65,97},{97,1},{2,34}... | collective-permute-start | bytes 55304 | tf_op jit(solution)/shard_map/ppermute | solution.py:50
  417.5 43.2 %collective-permute-start.34 = (bf16[8,1152]{1,0:T(8,128)(2,1)S(1)}, bf16[8,1152]{1,0:T(8,128)(2,1)S(1)}, u32[]{:S(2)}, u32[]{:S(2)}) collective-permute-start(bf16[8,1152]{1,0:T(8,128)(2,1)S(1)} %copy-done.40), channel_id=1, source_target_pairs={{0,64},{32,96},{64,0},{96,32},{1,65},{33,97},{65,1},{97,33},{2,66}... | collective-permute-start | bytes 55304 | tf_op jit(solution)/shard_map/ppermute | solution.py:50
  424.6 32.0 %collective-permute-start.27 = (f32[1,256]{1,0:T(1,128)S(1)}, f32[1,256]{1,0:T(1,128)S(1)}, u32[]{:S(2)}, u32[]{:S(2)}) collective-permute-start(f32[1,256]{1,0:T(1,128)S(1)} %get-tuple-element.102), channel_id=1, source_target_pairs={{0,1},{1,0},{2,3},{3,2},{4,5},{5,4},{6,7},{7,6},{8,9},{9,8},{10,11... | collective-permute-start | bytes 3080 | tf_op jit(solution)/shard_map/ppermute | solution.py:833
  424.7 32.0 %collective-permute-start.28 = (f32[1,256]{1,0:T(1,128)S(1)}, f32[1,256]{1,0:T(1,128)S(1)}, u32[]{:S(2)}, u32[]{:S(2)}) collective-permute-start(f32[1,256]{1,0:T(1,128)S(1)} %get-tuple-element.103), channel_id=1, source_target_pairs={{0,2},{1,3},{2,0},{3,1},{4,6},{5,7},{6,4},{7,5},{8,10},{9,11},{10,... | collective-permute-start | bytes 3080 | tf_op jit(solution)/shard_map/ppermute | solution.py:833
  446.9 11.2 %collective-permute-start.29 = (f32[1,256]{1,0:T(1,128)S(1)}, f32[1,256]{1,0:T(1,128)S(1)}, u32[]{:S(2)}, u32[]{:S(2)}) collective-permute-start(f32[1,256]{1,0:T(1,128)S(1)} %get-tuple-element.104), channel_id=1, source_target_pairs={{0,3},{1,2},{2,1},{3,0},{4,7},{5,6},{6,5},{7,4},{8,11},{9,10},{10,... | collective-permute-start | bytes 3080 | tf_op jit(solution)/shard_map/ppermute | solution.py:833
  448.0 14.3 %collective-permute-start.35 = (bf16[8,1152]{1,0:T(8,128)(2,1)S(1)}, bf16[8,1152]{1,0:T(8,128)(2,1)S(1)}, u32[]{:S(2)}, u32[]{:S(2)}) collective-permute-start(bf16[8,1152]{1,0:T(8,128)(2,1)S(1)} %copy-done.40), channel_id=1, source_target_pairs={{0,96},{32,0},{64,32},{96,64},{1,97},{33,1},{65,33},{97,65},{2,98}... | collective-permute-start | bytes 55304 | tf_op jit(solution)/shard_map/ppermute | solution.py:50
  456.7 13.3 %collective-permute-start.24 = (bf16[256,256]{1,0:T(8,128)(2,1)S(1)}, bf16[256,256]{1,0:T(8,128)(2,1)S(1)}, u32[]{:S(2)}, u32[]{:S(2)}) collective-permute-start(bf16[256,256]{1,0:T(8,128)(2,1)S(1)} %fusion.11.refs_1_), channel_id=1, source_target_pairs={{0,32},{32,64},{64,96},{96,0},{1,33},{33,65},{65,97},{97,1},{2,34}... | collective-permute-start | bytes 393224 | tf_op jit(solution)/shard_map/ppermute | solution.py:50
  456.7 13.9 %collective-permute-start.25 = (bf16[256,256]{1,0:T(8,128)(2,1)S(1)}, bf16[256,256]{1,0:T(8,128)(2,1)S(1)}, u32[]{:S(2)}, u32[]{:S(2)}) collective-permute-start(bf16[256,256]{1,0:T(8,128)(2,1)S(1)} %fusion.11.refs_1_), channel_id=1, source_target_pairs={{0,64},{32,96},{64,0},{96,32},{1,65},{33,97},{65,1},{97,33},{2,66}... | collective-permute-start | bytes 393224 | tf_op jit(solution)/shard_map/ppermute | solution.py:50
  458.2 13.1 %collective-permute-start.26 = (bf16[256,256]{1,0:T(8,128)(2,1)S(1)}, bf16[256,256]{1,0:T(8,128)(2,1)S(1)}, u32[]{:S(2)}, u32[]{:S(2)}) collective-permute-start(bf16[256,256]{1,0:T(8,128)(2,1)S(1)} %fusion.11.refs_1_), channel_id=1, source_target_pairs={{0,96},{32,0},{64,32},{96,64},{1,97},{33,1},{65,33},{97,65},{2,98}... | collective-permute-start | bytes 393224 | tf_op jit(solution)/shard_map/ppermute | solution.py:50
  461.3 5.1 collective-permute-start.30
  462.9 5.1 collective-permute-start.31
  466.4 3.6 collective-permute-start.32
  479.9 28.2 %all-to-all-start.9 = ((bf16[8,96,1152]{2,1,0:T(8,128)(2,1)}), bf16[8,96,1152]{2,1,0:T(8,128)(2,1)}, u32[]{:S(2)}, u32[]{:S(2)}) async-start(bf16[8,96,1152]{2,1,0:T(8,128)(2,1)} %copy-done.3), calls=%async_computation.9 | async-start | bytes 3538944 | tf_op jit(solution)/shard_map/all_to_all | solution.py:58
  (62 other events, 149.7 us)
